TPU v7x, 512 devices: a whole 4x8x8 slice. The times are simulated.
512 devices in a mesh: row: 16 (over x_hi, y), col: 8 (over z), layer: 4 (over x_lo, core).
Axes of the slice: x: 4 (x_hi: 2, x_lo: 2; x = x_hi * 2 + x_lo), y: 8, z: 8, core: 2. Of those that a mesh axis runs over, the one named last changes fastest.
Arguments:
- a_blocks: bfloat16 [16, 8, 4, 24, 128, 128], P('row', 'col', 'layer'), may hold values from -0.5 to 0.5
- a_index: int32 [16, 8, 4, 2, 24], P('row', 'col', 'layer'), may hold values from 0 to 511, as said below
- a_send: int32 [16, 8, 4, 8, 3], P('row', 'col', 'layer'), may hold values from 0 to 23, as said below
- a_count: int32 [16, 8, 4, 8], P('row', 'col', 'layer'), may hold values from 1 to 3, as said below
- b_blocks: bfloat16 [16, 8, 4, 16, 128, 128], P('row', 'col', 'layer'), may hold values from -6 to 6
- b_index: int32 [16, 8, 4, 2, 16], P('row', 'col', 'layer'), may hold values from 0 to 511, as said below
- b_send: int32 [16, 8, 4, 16, 2], P('row', 'col', 'layer'), may hold values from 0 to 15, as said below
- b_count: int32 [16, 8, 4, 16], P('row', 'col', 'layer'), may hold values from 0 to 2, as said below
- c_index: int32 [16, 8, 2, 24], P('row', 'col'), may hold values from 0 to 511, as said below
Outputs:
- product: bfloat16 [16, 8, 24, 128, 128], P('row', 'col', 'layer')
Inputs may be any that keep to these rules, and one draw needn't show every extreme that they name: `a_index`: every slot of a device is named by exactly one entry of its send lists. A slot named in list d of device (r, c, l) holds a block (i, k) with i % 16 = r, k % (32) = 8 * l + (r + d) % 8. `a_send`: each device's lists together name each of its 24 slots exactly once. `a_count`: in every draw some device receives 3 live blocks from every device of its row and layer. `b_index`: A slot named in list q of device (r, c, l) holds a block (k, j) with j % 8 = c and k % (32) = 8 * l + (q + c) % 8. No two live blocks of B share a position, and no block row of B holds more than 2 live blocks whose block columns are equal modulo 8; in every draw some such group holds 2. `b_send`: the lists of device (r, c, l) for rows q and q + 8 are equal, lists for rows that differ modulo 8 name disjoint slots, and together they name each of the 16 slots once. `b_count`: the counts for rows q and q + 8 are equal. In every draw some device receives 2 live blocks from every device of its column and layer. `c_index`: the kept blocks of cell (r, c) are distinct and have block row i with i % 16 = r and block column j with j % 8 = c.
All inputs are finite; a program needn't handle non-finite values.
Results may differ from a plain program's by a relative error of at most 0.012.
Values may be sent and summed in bfloat16 or wider, within the bound.
A program may use at most 128 MiB of HBM per device.

v0:
```python
import jax
import jax.numpy as jnp
from jax import lax
from jax.sharding import PartitionSpec as P

BLOCK = 128
B_MOST = 2


def passed_along(block, axis, distance):
    devices = range(lax.axis_size(axis))
    route = [((i - distance) % len(devices), i) for i in devices]
    return lax.ppermute(block, axis, route)


def outgoing(stored, indices, send_list, live_count):
    listed = stored[send_list]
    places = jnp.moveaxis(indices[:, send_list], 0, 1)
    live_flags = (lax.broadcasted_iota(jnp.int32, send_list.shape, 1) < live_count[:, None]).astype(
        jnp.int32
    )
    return (listed, places, live_flags)


def multiply(a_held, a_labels, bucket, b_labels, kept_rows, kept_cols, spread, running):
    k_band = a_labels[1] // spread
    picked = bucket[k_band]
    chosen = b_labels[k_band]
    found = (
        (a_labels[0][:, None, None] == kept_rows[None, None, :])
        & (chosen[:, 1][:, :, None] == kept_cols[None, None, :])
        & (chosen[:, 0][:, :, None] == a_labels[1][:, None, None])
        & (a_labels[2][:, None, None] > 0)
    )
    slot_count = kept_rows.shape[0]
    target = jnp.where(
        jnp.any(found, axis=2),
        jnp.sum(jnp.where(found, jnp.arange(slot_count, dtype=jnp.int32), 0), axis=2),
        slot_count,
    )
    products = jnp.einsum("amn,awnp->awmp", a_held, picked, preferred_element_type=jnp.float32)
    return running.at[target.reshape(-1)].add(
        products.reshape(-1, a_held.shape[1], a_held.shape[2]), mode="drop"
    )


def shards(a_blocks, a_index, a_send, a_count, b_blocks, b_index, b_send, b_count, c_index):
    col_count = lax.axis_size("col")
    spread = col_count * lax.axis_size("layer")
    a_list, a_places, a_live = outgoing(
        a_blocks[0, 0, 0], a_index[0, 0, 0], a_send[0, 0, 0], a_count[0, 0, 0]
    )
    a_list, a_places, a_live = (
        lax.all_to_all(a_list, "col", split_axis=0, concat_axis=0, tiled=True),
        lax.all_to_all(a_places, "col", split_axis=0, concat_axis=0, tiled=True),
        lax.all_to_all(a_live, "col", split_axis=0, concat_axis=0, tiled=True),
    )
    a_held = a_list.reshape(-1, BLOCK, BLOCK)
    a_labels = jnp.concatenate(
        [jnp.moveaxis(a_places, 1, 0).reshape(2, -1), a_live.reshape(1, -1)], axis=0
    )
    b_list, b_places, b_live = outgoing(
        b_blocks[0, 0, 0], b_index[0, 0, 0], b_send[0, 0, 0], b_count[0, 0, 0]
    )
    b_list, b_places, b_live = (
        lax.all_to_all(b_list, "row", split_axis=0, concat_axis=0, tiled=True),
        lax.all_to_all(b_places, "row", split_axis=0, concat_axis=0, tiled=True),
        lax.all_to_all(b_live, "row", split_axis=0, concat_axis=0, tiled=True),
    )
    received = b_list.reshape(-1, BLOCK, BLOCK)
    places = jnp.moveaxis(b_places, 1, 0).reshape(2, -1)
    b_flags = b_live.reshape(-1)
    spot_count = received.shape[0]
    position = jnp.arange(spot_count, dtype=jnp.int32)
    k_band = places[0] // spread
    before = (
        (k_band[None, :] == k_band[:, None])
        & (b_flags[None, :] > 0)
        & (position[None, :] < position[:, None])
    )
    b_rank = jnp.sum(before.astype(jnp.int32), axis=1)
    target = jnp.where(b_flags > 0, k_band * B_MOST + b_rank, spot_count)
    b_hit = target[None, :] == position[:, None]
    source = jnp.sum(jnp.where(b_hit, position[None, :], 0), axis=1)
    filled = jnp.any(b_hit, axis=1)
    bucket = received[source].reshape(-1, B_MOST, BLOCK, BLOCK)
    b_labels = jnp.stack([places[0][source], jnp.where(filled, places[1][source], -1)]).reshape(
        2, -1, B_MOST
    )
    b_labels = jnp.moveaxis(b_labels, 0, 1)
    kept_rows = c_index[0, 0, 0]
    kept_cols = c_index[0, 0, 1]
    running = jnp.zeros((kept_rows.shape[0], BLOCK, BLOCK), jnp.float32)
    running = multiply(a_held, a_labels, bucket, b_labels, kept_rows, kept_cols, spread, running)

    def advance(turn_index, loop_state):
        moving_blocks, moving_labels, moving_bucket, moving_marks, running = loop_state
        moving_blocks, moving_labels = passed_along((moving_blocks, moving_labels), "col", -1)
        moving_bucket, moving_marks = passed_along((moving_bucket, moving_marks), "row", -1)
        running = multiply(
            moving_blocks,
            moving_labels,
            moving_bucket,
            moving_marks,
            kept_rows,
            kept_cols,
            spread,
            running,
        )
        return (moving_blocks, moving_labels, moving_bucket, moving_marks, running)

    loop_state = lax.fori_loop(
        0, col_count - 1, advance, (a_held, a_labels, bucket, b_labels, running)
    )
    running = loop_state[4]
    result = lax.psum_scatter(
        running.astype(jnp.bfloat16), "layer", scatter_dimension=0, tiled=True
    )
    return result[None, None]


def solution(mesh):
    in_specs = (
        P("row", "col", "layer", None, None, None),
        P("row", "col", "layer", None, None),
        P("row", "col", "layer", None, None),
        P("row", "col", "layer", None),
        P("row", "col", "layer", None, None, None),
        P("row", "col", "layer", None, None),
        P("row", "col", "layer", None, None),
        P("row", "col", "layer", None),
        P("row", "col", None, None),
    )
    out_specs = P("row", "col", "layer", None, None)
    return jax.shard_map(shards, mesh=mesh, in_specs=in_specs, out_specs=out_specs, check_vma=False)
```

profile of v0, /device:TPU:1, one launch (start us, length us, event | category | flops | bytes accessed | tf_op | source)
XLA Modules:
  0.0 505.9 jit_solution(6308912347433699399)
XLA Ops:
  8.0 10.9 %all-to-all-start.2 = ((s32[8,1,3]{2,1,0:T(1,128)}), s32[8,1,3]{2,1,0:T(1,128)S(1)}, u32[]{:S(2)}, u32[]{:S(2)}) async-start(s32[8,1,3]{2,1,0:T(1,128)} %compare_convert_fusion.1), calls=%async_computation.2 | async-start | bytes 8192 | tf_op jit(solution)/shard_map/all_to_all | solution.py:56
  26.9 9.4 %all-to-all-start.4 = ((s32[16,1,2]{2,1,0:T(1,128)}), s32[16,1,2]{2,1,0:T(1,128)S(1)}, u32[]{:S(2)}, u32[]{:S(2)}) async-start(s32[16,1,2]{2,1,0:T(1,128)} %compare_convert_fusion), calls=%async_computation.4 | async-start | bytes 16384 | tf_op jit(solution)/shard_map/all_to_all | solution.py:68
  45.1 6.6 %all-to-all-start.1 = ((s32[8,2,3]{2,1,0:T(2,128)}), s32[8,2,3]{2,1,0:T(2,128)S(1)}, u32[]{:S(2)}, u32[]{:S(2)}) async-start(s32[8,2,3]{2,1,0:T(2,128)} %copy.79), calls=%async_computation.1 | async-start | bytes 16384 | tf_op jit(solution)/shard_map/all_to_all | solution.py:55
  62.0 8.7 %all-to-all-done.5 = s32[16,2,2]{2,1,0:T(2,128)S(1)} async-done(((s32[16,2,2]{2,1,0:T(2,128)}), s32[16,2,2]{2,1,0:T(2,128)S(1)}, u32[]{:S(2)}, u32[]{:S(2)}) %all-to-all-start.5) | async-done | bytes 288 | tf_op jit(solution)/shard_map/all_to_all | solution.py:67
  77.0 19.2 %all-to-all-done.3 = bf16[16,2,128,128]{3,2,1,0:T(8,128)(2,1)S(1)} async-done(((bf16[16,2,128,128]{3,2,1,0:T(8,128)(2,1)}), bf16[16,2,128,128]{3,2,1,0:T(8,128)(2,1)S(1)}, u32[]{:S(2)}, u32[]{:S(2)}) %all-to-all-start.3) | async-done | bytes 1048608 | tf_op jit(solution)/shard_map/all_to_all | solution.py:66
  103.7 10.8 %all-to-all-done = bf16[8,3,128,128]{3,2,1,0:T(8,128)(2,1)} async-done(((bf16[8,3,128,128]{3,2,1,0:T(8,128)(2,1)}), bf16[8,3,128,128]{3,2,1,0:T(8,128)(2,1)}, u32[]{:S(2)}, u32[]{:S(2)}) %all-to-all-start) | async-done | bytes 786464 | tf_op jit(solution)/shard_map/all_to_all | solution.py:54
  121.8 6.7 %scatter_fusion.1 = f32[24,128,128]{2,1,0:T(8,128)S(1)} fusion(f32[24,128,128]{2,1,0:T(8,128)S(1)} %broadcast_in_dim.68, s32[48]{0:T(128)S(1)} %fusion.10, f32[48,128,128]{2,1,0:T(8,128)} %copy.91), kind=kCustom, calls=%fused_computation.12 | custom fusion | flops 786432 | bytes 9437376 | tf_op jit(solution)/shard_map/scatter-add | solution.py:42
  128.5 340.3 %while.20 = (s32[]{:T(128)}, bf16[24,128,128]{2,1,0:T(8,128)(2,1)}, s32[3,24]{1,0:T(4,128)S(1)}, bf16[16,2,128,128]{3,2,1,0:T(8,128)(2,1)}, s32[16,2,2]{2,1,0:T(...) while((s32[]{:T(128)}, bf16[24,128,128]{2,1,0:T(8,128)(2,1)}, ...), condition=%wide.region_10.11_spmd, body=%wide.region_6.10_spmd.sunk | while | flops 202127904 | bytes 35405332 | solution.py:112
  130.4 12.5 %collective-permute-start.3 = (s32[16,2,2]{2,1,0:T(2,128)S(1)}, s32[16,2,2]{2,1,0:T(2,128)S(1)}, u32[]{:S(2)}, u32[]{:S(2)}) collective-permute-start(s32[16,2,2]{2,1,0:T(2,128)S(1)} %get-tuple-element.217), channel_id=1, source_target_pairs={{32,0},{64,32},{96,64},{128,96},{160,128},{192,160},{224,192},{256... | collective-permute-start | bytes 776 | tf_op jit(solution)/shard_map/while/body/eval_jaxpr/ppermute | solution.py:13
  149.0 10.9 %collective-permute-done = bf16[24,128,128]{2,1,0:T(8,128)(2,1)} collective-permute-done((bf16[24,128,128]{2,1,0:T(8,128)(2,1)}, bf16[24,128,128]{2,1,0:T(8,128)(2,1)}, u32[]{:S(2)}, u32[]{:S(2)}) %collective-permute-start) | collective-permute-done | bytes 786464 | tf_op jit(solution)/shard_map/while/body/eval_jaxpr/ppermute | solution.py:13
  176.9 6.7 %scatter_fusion = f32[24,128,128]{2,1,0:T(8,128)S(1)} fusion(f32[24,128,128]{2,1,0:T(8,128)S(1)} %get-tuple-element.218, s32[48]{0:T(128)S(1)} %fusion.30, f32[48,128,128]{2,1,0:T(8,128)} %copy.104), kind=kCustom, calls=%fused_computation.11.clone.1 | custom fusion | flops 786432 | bytes 9437376 | tf_op jit(solution)/shard_map/while/body/eval_jaxpr/scatter-add | solution.py:42
  186.5 5.7 %collective-permute-start.3 = (s32[16,2,2]{2,1,0:T(2,128)S(1)}, s32[16,2,2]{2,1,0:T(2,128)S(1)}, u32[]{:S(2)}, u32[]{:S(2)}) collective-permute-start(s32[16,2,2]{2,1,0:T(2,128)S(1)} %get-tuple-element.217), channel_id=1, source_target_pairs={{32,0},{64,32},{96,64},{128,96},{160,128},{192,160},{224,192},{256... | collective-permute-start | bytes 776 | tf_op jit(solution)/shard_map/while/body/eval_jaxpr/ppermute | solution.py:13
  197.7 9.6 %collective-permute-done = bf16[24,128,128]{2,1,0:T(8,128)(2,1)} collective-permute-done((bf16[24,128,128]{2,1,0:T(8,128)(2,1)}, bf16[24,128,128]{2,1,0:T(8,128)(2,1)}, u32[]{:S(2)}, u32[]{:S(2)}) %collective-permute-start) | collective-permute-done | bytes 786464 | tf_op jit(solution)/shard_map/while/body/eval_jaxpr/ppermute | solution.py:13
  223.9 6.7 %scatter_fusion = f32[24,128,128]{2,1,0:T(8,128)S(1)} fusion(f32[24,128,128]{2,1,0:T(8,128)S(1)} %get-tuple-element.218, s32[48]{0:T(128)S(1)} %fusion.30, f32[48,128,128]{2,1,0:T(8,128)} %copy.104), kind=kCustom, calls=%fused_computation.11.clone.1 | custom fusion | flops 786432 | bytes 9437376 | tf_op jit(solution)/shard_map/while/body/eval_jaxpr/scatter-add | solution.py:42
  231.6 6.5 %collective-permute-start.1 = (s32[3,24]{1,0:T(4,128)S(1)}, s32[3,24]{1,0:T(4,128)S(1)}, u32[]{:S(2)}, u32[]{:S(2)}) collective-permute-start(s32[3,24]{1,0:T(4,128)S(1)} %get-tuple-element.215), channel_id=1, source_target_pairs={{4,0},{8,4},{12,8},{16,12},{20,16},{24,20},{28,24},{0,28},{5,1},{9... | collective-permute-start | bytes 872 | tf_op jit(solution)/shard_map/while/body/eval_jaxpr/ppermute | solution.py:13
  238.1 5.8 %collective-permute-start.3 = (s32[16,2,2]{2,1,0:T(2,128)S(1)}, s32[16,2,2]{2,1,0:T(2,128)S(1)}, u32[]{:S(2)}, u32[]{:S(2)}) collective-permute-start(s32[16,2,2]{2,1,0:T(2,128)S(1)} %get-tuple-element.217), channel_id=1, source_target_pairs={{32,0},{64,32},{96,64},{128,96},{160,128},{192,160},{224,192},{256... | collective-permute-start | bytes 776 | tf_op jit(solution)/shard_map/while/body/eval_jaxpr/ppermute | solution.py:13
  251.3 7.1 %collective-permute-done = bf16[24,128,128]{2,1,0:T(8,128)(2,1)} collective-permute-done((bf16[24,128,128]{2,1,0:T(8,128)(2,1)}, bf16[24,128,128]{2,1,0:T(8,128)(2,1)}, u32[]{:S(2)}, u32[]{:S(2)}) %collective-permute-start) | collective-permute-done | bytes 786464 | tf_op jit(solution)/shard_map/while/body/eval_jaxpr/ppermute | solution.py:13
  260.5 7.3 %collective-permute-done.2 = bf16[16,2,128,128]{3,2,1,0:T(8,128)(2,1)S(1)} collective-permute-done((bf16[16,2,128,128]{3,2,1,0:T(8,128)(2,1)}, bf16[16,2,128,128]{3,2,1,0:T(8,128)(2,1)S(1)}, u32[]{:S(2)}, u32[]{:S(2)}) %collective-permute-start.2) | collective-permute-done | bytes 1048608 | tf_op jit(solution)/shard_map/while/body/eval_jaxpr/ppermute | solution.py:13
  277.2 6.7 %scatter_fusion = f32[24,128,128]{2,1,0:T(8,128)S(1)} fusion(f32[24,128,128]{2,1,0:T(8,128)S(1)} %get-tuple-element.218, s32[48]{0:T(128)S(1)} %fusion.30, f32[48,128,128]{2,1,0:T(8,128)} %copy.104), kind=kCustom, calls=%fused_computation.11.clone.1 | custom fusion | flops 786432 | bytes 9437376 | tf_op jit(solution)/shard_map/while/body/eval_jaxpr/scatter-add | solution.py:42
  287.4 6.1 %collective-permute-start.3 = (s32[16,2,2]{2,1,0:T(2,128)S(1)}, s32[16,2,2]{2,1,0:T(2,128)S(1)}, u32[]{:S(2)}, u32[]{:S(2)}) collective-permute-start(s32[16,2,2]{2,1,0:T(2,128)S(1)} %get-tuple-element.217), channel_id=1, source_target_pairs={{32,0},{64,32},{96,64},{128,96},{160,128},{192,160},{224,192},{256... | collective-permute-start | bytes 776 | tf_op jit(solution)/shard_map/while/body/eval_jaxpr/ppermute | solution.py:13
  298.9 8.2 %collective-permute-done = bf16[24,128,128]{2,1,0:T(8,128)(2,1)} collective-permute-done((bf16[24,128,128]{2,1,0:T(8,128)(2,1)}, bf16[24,128,128]{2,1,0:T(8,128)(2,1)}, u32[]{:S(2)}, u32[]{:S(2)}) %collective-permute-start) | collective-permute-done | bytes 786464 | tf_op jit(solution)/shard_map/while/body/eval_jaxpr/ppermute | solution.py:13
  324.1 6.7 %scatter_fusion = f32[24,128,128]{2,1,0:T(8,128)S(1)} fusion(f32[24,128,128]{2,1,0:T(8,128)S(1)} %get-tuple-element.218, s32[48]{0:T(128)S(1)} %fusion.30, f32[48,128,128]{2,1,0:T(8,128)} %copy.104), kind=kCustom, calls=%fused_computation.11.clone.1 | custom fusion | flops 786432 | bytes 9437376 | tf_op jit(solution)/shard_map/while/body/eval_jaxpr/scatter-add | solution.py:42
  333.7 5.7 %collective-permute-start.3 = (s32[16,2,2]{2,1,0:T(2,128)S(1)}, s32[16,2,2]{2,1,0:T(2,128)S(1)}, u32[]{:S(2)}, u32[]{:S(2)}) collective-permute-start(s32[16,2,2]{2,1,0:T(2,128)S(1)} %get-tuple-element.217), channel_id=1, source_target_pairs={{32,0},{64,32},{96,64},{128,96},{160,128},{192,160},{224,192},{256... | collective-permute-start | bytes 776 | tf_op jit(solution)/shard_map/while/body/eval_jaxpr/ppermute | solution.py:13
  344.9 7.7 %collective-permute-done = bf16[24,128,128]{2,1,0:T(8,128)(2,1)} collective-permute-done((bf16[24,128,128]{2,1,0:T(8,128)(2,1)}, bf16[24,128,128]{2,1,0:T(8,128)(2,1)}, u32[]{:S(2)}, u32[]{:S(2)}) %collective-permute-start) | collective-permute-done | bytes 786464 | tf_op jit(solution)/shard_map/while/body/eval_jaxpr/ppermute | solution.py:13
  369.1 6.7 %scatter_fusion = f32[24,128,128]{2,1,0:T(8,128)S(1)} fusion(f32[24,128,128]{2,1,0:T(8,128)S(1)} %get-tuple-element.218, s32[48]{0:T(128)S(1)} %fusion.30, f32[48,128,128]{2,1,0:T(8,128)} %copy.104), kind=kCustom, calls=%fused_computation.11.clone.1 | custom fusion | flops 786432 | bytes 9437376 | tf_op jit(solution)/shard_map/while/body/eval_jaxpr/scatter-add | solution.py:42
  378.7 5.7 %collective-permute-start.3 = (s32[16,2,2]{2,1,0:T(2,128)S(1)}, s32[16,2,2]{2,1,0:T(2,128)S(1)}, u32[]{:S(2)}, u32[]{:S(2)}) collective-permute-start(s32[16,2,2]{2,1,0:T(2,128)S(1)} %get-tuple-element.217), channel_id=1, source_target_pairs={{32,0},{64,32},{96,64},{128,96},{160,128},{192,160},{224,192},{256... | collective-permute-start | bytes 776 | tf_op jit(solution)/shard_map/while/body/eval_jaxpr/ppermute | solution.py:13
  389.8 7.7 %collective-permute-done = bf16[24,128,128]{2,1,0:T(8,128)(2,1)} collective-permute-done((bf16[24,128,128]{2,1,0:T(8,128)(2,1)}, bf16[24,128,128]{2,1,0:T(8,128)(2,1)}, u32[]{:S(2)}, u32[]{:S(2)}) %collective-permute-start) | collective-permute-done | bytes 786464 | tf_op jit(solution)/shard_map/while/body/eval_jaxpr/ppermute | solution.py:13
  413.2 6.7 %scatter_fusion = f32[24,128,128]{2,1,0:T(8,128)S(1)} fusion(f32[24,128,128]{2,1,0:T(8,128)S(1)} %get-tuple-element.218, s32[48]{0:T(128)S(1)} %fusion.30, f32[48,128,128]{2,1,0:T(8,128)} %copy.104), kind=kCustom, calls=%fused_computation.11.clone.1 | custom fusion | flops 786432 | bytes 9437376 | tf_op jit(solution)/shard_map/while/body/eval_jaxpr/scatter-add | solution.py:42
  429.1 6.1 %collective-permute-start = (bf16[24,128,128]{2,1,0:T(8,128)(2,1)}, bf16[24,128,128]{2,1,0:T(8,128)(2,1)}, u32[]{:S(2)}, u32[]{:S(2)}) collective-permute-start(bf16[24,128,128]{2,1,0:T(8,128)(2,1)} %get-tuple-element.214), channel_id=1, source_target_pairs={{4,0},{8,4},{12,8},{16,12},{20,16},{24,20},{28,24},{0,28},{5,1},{9... | collective-permute-start | bytes 2359304 | tf_op jit(solution)/shard_map/while/body/eval_jaxpr/ppermute | solution.py:13
  438.8 5.8 %collective-permute-done = bf16[24,128,128]{2,1,0:T(8,128)(2,1)} collective-permute-done((bf16[24,128,128]{2,1,0:T(8,128)(2,1)}, bf16[24,128,128]{2,1,0:T(8,128)(2,1)}, u32[]{:S(2)}, u32[]{:S(2)}) %collective-permute-start) | collective-permute-done | bytes 786464 | tf_op jit(solution)/shard_map/while/body/eval_jaxpr/ppermute | solution.py:13
  461.0 6.7 %scatter_fusion = f32[24,128,128]{2,1,0:T(8,128)S(1)} fusion(f32[24,128,128]{2,1,0:T(8,128)S(1)} %get-tuple-element.218, s32[48]{0:T(128)S(1)} %fusion.30, f32[48,128,128]{2,1,0:T(8,128)} %copy.104), kind=kCustom, calls=%fused_computation.11.clone.1 | custom fusion | flops 786432 | bytes 9437376 | tf_op jit(solution)/shard_map/while/body/eval_jaxpr/scatter-add | solution.py:42
  469.8 29.3 %reduce-scatter.2.cloned.1.call-done = bf16[6,128,128]{2,1,0:T(8,128)(2,1)} async-done(((bf16[24,128,128]{2,1,0:T(8,128)(2,1)}), bf16[6,128,128]{2,1,0:T(8,128)(2,1)}) %reduce-scatter.2.cloned.1.call-update) | async-done | bytes 196624 | tf_op jit(solution)/shard_map/reduce_scatter | solution.py:116
  (287 shorter events, 224.6 us)
Async XLA Ops:
  8.0 18.9 %all-to-all-start.2 = ((s32[8,1,3]{2,1,0:T(1,128)}), s32[8,1,3]{2,1,0:T(1,128)S(1)}, u32[]{:S(2)}, u32[]{:S(2)}) async-start(s32[8,1,3]{2,1,0:T(1,128)} %compare_convert_fusion.1), calls=%async_computation.2 | async-start | bytes 8192 | tf_op jit(solution)/shard_map/all_to_all | solution.py:56
  26.9 18.2 %all-to-all-start.4 = ((s32[16,1,2]{2,1,0:T(1,128)}), s32[16,1,2]{2,1,0:T(1,128)S(1)}, u32[]{:S(2)}, u32[]{:S(2)}) async-start(s32[16,1,2]{2,1,0:T(1,128)} %compare_convert_fusion), calls=%async_computation.4 | async-start | bytes 16384 | tf_op jit(solution)/shard_map/all_to_all | solution.py:68
  45.1 13.2 %all-to-all-start.1 = ((s32[8,2,3]{2,1,0:T(2,128)}), s32[8,2,3]{2,1,0:T(2,128)S(1)}, u32[]{:S(2)}, u32[]{:S(2)}) async-start(s32[8,2,3]{2,1,0:T(2,128)} %copy.79), calls=%async_computation.1 | async-start | bytes 16384 | tf_op jit(solution)/shard_map/all_to_all | solution.py:55
  58.3 12.4 %all-to-all-start.5 = ((s32[16,2,2]{2,1,0:T(2,128)}), s32[16,2,2]{2,1,0:T(2,128)S(1)}, u32[]{:S(2)}, u32[]{:S(2)}) async-start(s32[16,2,2]{2,1,0:T(2,128)} %copy.84), calls=%async_computation.5 | async-start | bytes 32768 | tf_op jit(solution)/shard_map/all_to_all | solution.py:67
  70.7 25.5 %all-to-all-start.3 = ((bf16[16,2,128,128]{3,2,1,0:T(8,128)(2,1)}), bf16[16,2,128,128]{3,2,1,0:T(8,128)(2,1)S(1)}, u32[]{:S(2)}, u32[]{:S(2)}) async-start(bf16[16,2,128,128]{3,2,1,0:T(8,128)(2,1)} %bitcast.24), calls=%async_computation.3 | async-start | bytes 2097152 | tf_op jit(solution)/shard_map/all_to_all | solution.py:66
  96.2 18.4 %all-to-all-start = ((bf16[8,3,128,128]{3,2,1,0:T(8,128)(2,1)}), bf16[8,3,128,128]{3,2,1,0:T(8,128)(2,1)}, u32[]{:S(2)}, u32[]{:S(2)}) async-start(bf16[8,3,128,128]{3,2,1,0:T(8,128)(2,1)} %bitcast.16), calls=%async_computation | async-start | bytes 1572864 | tf_op jit(solution)/shard_map/all_to_all | solution.py:54
  100.4 398.7 %reduce-scatter.2.cloned.1.call-start = ((), (), s32[]{:S(2)}) async-start(), calls=%async_computation.7 | async-start | bytes 983040 | tf_op jit(solution)/shard_map/reduce_scatter | solution.py:116
  128.5 18.9 %collective-permute-start.1 = (s32[3,24]{1,0:T(4,128)S(1)}, s32[3,24]{1,0:T(4,128)S(1)}, u32[]{:S(2)}, u32[]{:S(2)}) collective-permute-start(s32[3,24]{1,0:T(4,128)S(1)} %get-tuple-element.215), channel_id=1, source_target_pairs={{4,0},{8,4},{12,8},{16,12},{20,16},{24,20},{28,24},{0,28},{5,1},{9... | collective-permute-start | bytes 872 | tf_op jit(solution)/shard_map/while/body/eval_jaxpr/ppermute | solution.py:13
  130.4 17.0 %collective-permute-start.3 = (s32[16,2,2]{2,1,0:T(2,128)S(1)}, s32[16,2,2]{2,1,0:T(2,128)S(1)}, u32[]{:S(2)}, u32[]{:S(2)}) collective-permute-start(s32[16,2,2]{2,1,0:T(2,128)S(1)} %get-tuple-element.217), channel_id=1, source_target_pairs={{32,0},{64,32},{96,64},{128,96},{160,128},{192,160},{224,192},{256... | collective-permute-start | bytes 776 | tf_op jit(solution)/shard_map/while/body/eval_jaxpr/ppermute | solution.py:13
  143.0 16.9 %collective-permute-start = (bf16[24,128,128]{2,1,0:T(8,128)(2,1)}, bf16[24,128,128]{2,1,0:T(8,128)(2,1)}, u32[]{:S(2)}, u32[]{:S(2)}) collective-permute-start(bf16[24,128,128]{2,1,0:T(8,128)(2,1)} %get-tuple-element.214), channel_id=1, source_target_pairs={{4,0},{8,4},{12,8},{16,12},{20,16},{24,20},{28,24},{0,28},{5,1},{9... | collective-permute-start | bytes 2359304 | tf_op jit(solution)/shard_map/while/body/eval_jaxpr/ppermute | solution.py:13
  145.5 22.0 %collective-permute-start.2 = (bf16[16,2,128,128]{3,2,1,0:T(8,128)(2,1)}, bf16[16,2,128,128]{3,2,1,0:T(8,128)(2,1)S(1)}, u32[]{:S(2)}, u32[]{:S(2)}) collective-permute-start(bf16[16,2,128,128]{3,2,1,0:T(8,128)(2,1)} %get-tuple-element.216), channel_id=1, source_target_pairs={{32,0},{64,32},{96,64},{128,96},{160,128},{192,160},{224,192},{256... | collective-permute-start | bytes 3145736 | tf_op jit(solution)/shard_map/while/body/eval_jaxpr/ppermute | solution.py:13
  184.6 11.5 %collective-permute-start.1 = (s32[3,24]{1,0:T(4,128)S(1)}, s32[3,24]{1,0:T(4,128)S(1)}, u32[]{:S(2)}, u32[]{:S(2)}) collective-permute-start(s32[3,24]{1,0:T(4,128)S(1)} %get-tuple-element.215), channel_id=1, source_target_pairs={{4,0},{8,4},{12,8},{16,12},{20,16},{24,20},{28,24},{0,28},{5,1},{9... | collective-permute-start | bytes 872 | tf_op jit(solution)/shard_map/while/body/eval_jaxpr/ppermute | solution.py:13
  192.3 15.0 %collective-permute-start = (bf16[24,128,128]{2,1,0:T(8,128)(2,1)}, bf16[24,128,128]{2,1,0:T(8,128)(2,1)}, u32[]{:S(2)}, u32[]{:S(2)}) collective-permute-start(bf16[24,128,128]{2,1,0:T(8,128)(2,1)} %get-tuple-element.214), channel_id=1, source_target_pairs={{4,0},{8,4},{12,8},{16,12},{20,16},{24,20},{28,24},{0,28},{5,1},{9... | collective-permute-start | bytes 2359304 | tf_op jit(solution)/shard_map/while/body/eval_jaxpr/ppermute | solution.py:13
  194.2 20.3 %collective-permute-start.2 = (bf16[16,2,128,128]{3,2,1,0:T(8,128)(2,1)}, bf16[16,2,128,128]{3,2,1,0:T(8,128)(2,1)S(1)}, u32[]{:S(2)}, u32[]{:S(2)}) collective-permute-start(bf16[16,2,128,128]{3,2,1,0:T(8,128)(2,1)} %get-tuple-element.216), channel_id=1, source_target_pairs={{32,0},{64,32},{96,64},{128,96},{160,128},{192,160},{224,192},{256... | collective-permute-start | bytes 3145736 | tf_op jit(solution)/shard_map/while/body/eval_jaxpr/ppermute | solution.py:13
  231.6 18.2 %collective-permute-start.1 = (s32[3,24]{1,0:T(4,128)S(1)}, s32[3,24]{1,0:T(4,128)S(1)}, u32[]{:S(2)}, u32[]{:S(2)}) collective-permute-start(s32[3,24]{1,0:T(4,128)S(1)} %get-tuple-element.215), channel_id=1, source_target_pairs={{4,0},{8,4},{12,8},{16,12},{20,16},{24,20},{28,24},{0,28},{5,1},{9... | collective-permute-start | bytes 872 | tf_op jit(solution)/shard_map/while/body/eval_jaxpr/ppermute | solution.py:13
  238.1 11.7 %collective-permute-start.3 = (s32[16,2,2]{2,1,0:T(2,128)S(1)}, s32[16,2,2]{2,1,0:T(2,128)S(1)}, u32[]{:S(2)}, u32[]{:S(2)}) collective-permute-start(s32[16,2,2]{2,1,0:T(2,128)S(1)} %get-tuple-element.217), channel_id=1, source_target_pairs={{32,0},{64,32},{96,64},{128,96},{160,128},{192,160},{224,192},{256... | collective-permute-start | bytes 776 | tf_op jit(solution)/shard_map/while/body/eval_jaxpr/ppermute | solution.py:13
  243.9 14.5 %collective-permute-start = (bf16[24,128,128]{2,1,0:T(8,128)(2,1)}, bf16[24,128,128]{2,1,0:T(8,128)(2,1)}, u32[]{:S(2)}, u32[]{:S(2)}) collective-permute-start(bf16[24,128,128]{2,1,0:T(8,128)(2,1)} %get-tuple-element.214), channel_id=1, source_target_pairs={{4,0},{8,4},{12,8},{16,12},{20,16},{24,20},{28,24},{0,28},{5,1},{9... | collective-permute-start | bytes 2359304 | tf_op jit(solution)/shard_map/while/body/eval_jaxpr/ppermute | solution.py:13
  247.8 19.9 %collective-permute-start.2 = (bf16[16,2,128,128]{3,2,1,0:T(8,128)(2,1)}, bf16[16,2,128,128]{3,2,1,0:T(8,128)(2,1)S(1)}, u32[]{:S(2)}, u32[]{:S(2)}) collective-permute-start(bf16[16,2,128,128]{3,2,1,0:T(8,128)(2,1)} %get-tuple-element.216), channel_id=1, source_target_pairs={{32,0},{64,32},{96,64},{128,96},{160,128},{192,160},{224,192},{256... | collective-permute-start | bytes 3145736 | tf_op jit(solution)/shard_map/while/body/eval_jaxpr/ppermute | solution.py:13
  284.9 12.5 %collective-permute-start.1 = (s32[3,24]{1,0:T(4,128)S(1)}, s32[3,24]{1,0:T(4,128)S(1)}, u32[]{:S(2)}, u32[]{:S(2)}) collective-permute-start(s32[3,24]{1,0:T(4,128)S(1)} %get-tuple-element.215), channel_id=1, source_target_pairs={{4,0},{8,4},{12,8},{16,12},{20,16},{24,20},{28,24},{0,28},{5,1},{9... | collective-permute-start | bytes 872 | tf_op jit(solution)/shard_map/while/body/eval_jaxpr/ppermute | solution.py:13
  287.4 9.9 %collective-permute-start.3 = (s32[16,2,2]{2,1,0:T(2,128)S(1)}, s32[16,2,2]{2,1,0:T(2,128)S(1)}, u32[]{:S(2)}, u32[]{:S(2)}) collective-permute-start(s32[16,2,2]{2,1,0:T(2,128)S(1)} %get-tuple-element.217), channel_id=1, source_target_pairs={{32,0},{64,32},{96,64},{128,96},{160,128},{192,160},{224,192},{256... | collective-permute-start | bytes 776 | tf_op jit(solution)/shard_map/while/body/eval_jaxpr/ppermute | solution.py:13
  293.5 13.6 %collective-permute-start = (bf16[24,128,128]{2,1,0:T(8,128)(2,1)}, bf16[24,128,128]{2,1,0:T(8,128)(2,1)}, u32[]{:S(2)}, u32[]{:S(2)}) collective-permute-start(bf16[24,128,128]{2,1,0:T(8,128)(2,1)} %get-tuple-element.214), channel_id=1, source_target_pairs={{4,0},{8,4},{12,8},{16,12},{20,16},{24,20},{28,24},{0,28},{5,1},{9... | collective-permute-start | bytes 2359304 | tf_op jit(solution)/shard_map/while/body/eval_jaxpr/ppermute | solution.py:13
  295.4 19.2 %collective-permute-start.2 = (bf16[16,2,128,128]{3,2,1,0:T(8,128)(2,1)}, bf16[16,2,128,128]{3,2,1,0:T(8,128)(2,1)S(1)}, u32[]{:S(2)}, u32[]{:S(2)}) collective-permute-start(bf16[16,2,128,128]{3,2,1,0:T(8,128)(2,1)} %get-tuple-element.216), channel_id=1, source_target_pairs={{32,0},{64,32},{96,64},{128,96},{160,128},{192,160},{224,192},{256... | collective-permute-start | bytes 3145736 | tf_op jit(solution)/shard_map/while/body/eval_jaxpr/ppermute | solution.py:13
  331.8 11.5 %collective-permute-start.1 = (s32[3,24]{1,0:T(4,128)S(1)}, s32[3,24]{1,0:T(4,128)S(1)}, u32[]{:S(2)}, u32[]{:S(2)}) collective-permute-start(s32[3,24]{1,0:T(4,128)S(1)} %get-tuple-element.215), channel_id=1, source_target_pairs={{4,0},{8,4},{12,8},{16,12},{20,16},{24,20},{28,24},{0,28},{5,1},{9... | collective-permute-start | bytes 872 | tf_op jit(solution)/shard_map/while/body/eval_jaxpr/ppermute | solution.py:13
  339.5 13.1 %collective-permute-start = (bf16[24,128,128]{2,1,0:T(8,128)(2,1)}, bf16[24,128,128]{2,1,0:T(8,128)(2,1)}, u32[]{:S(2)}, u32[]{:S(2)}) collective-permute-start(bf16[24,128,128]{2,1,0:T(8,128)(2,1)} %get-tuple-element.214), channel_id=1, source_target_pairs={{4,0},{8,4},{12,8},{16,12},{20,16},{24,20},{28,24},{0,28},{5,1},{9... | collective-permute-start | bytes 2359304 | tf_op jit(solution)/shard_map/while/body/eval_jaxpr/ppermute | solution.py:13
  341.4 18.2 %collective-permute-start.2 = (bf16[16,2,128,128]{3,2,1,0:T(8,128)(2,1)}, bf16[16,2,128,128]{3,2,1,0:T(8,128)(2,1)S(1)}, u32[]{:S(2)}, u32[]{:S(2)}) collective-permute-start(bf16[16,2,128,128]{3,2,1,0:T(8,128)(2,1)} %get-tuple-element.216), channel_id=1, source_target_pairs={{32,0},{64,32},{96,64},{128,96},{160,128},{192,160},{224,192},{256... | collective-permute-start | bytes 3145736 | tf_op jit(solution)/shard_map/while/body/eval_jaxpr/ppermute | solution.py:13
  376.8 11.5 %collective-permute-start.1 = (s32[3,24]{1,0:T(4,128)S(1)}, s32[3,24]{1,0:T(4,128)S(1)}, u32[]{:S(2)}, u32[]{:S(2)}) collective-permute-start(s32[3,24]{1,0:T(4,128)S(1)} %get-tuple-element.215), channel_id=1, source_target_pairs={{4,0},{8,4},{12,8},{16,12},{20,16},{24,20},{28,24},{0,28},{5,1},{9... | collective-permute-start | bytes 872 | tf_op jit(solution)/shard_map/while/body/eval_jaxpr/ppermute | solution.py:13
  384.4 13.1 %collective-permute-start = (bf16[24,128,128]{2,1,0:T(8,128)(2,1)}, bf16[24,128,128]{2,1,0:T(8,128)(2,1)}, u32[]{:S(2)}, u32[]{:S(2)}) collective-permute-start(bf16[24,128,128]{2,1,0:T(8,128)(2,1)} %get-tuple-element.214), channel_id=1, source_target_pairs={{4,0},{8,4},{12,8},{16,12},{20,16},{24,20},{28,24},{0,28},{5,1},{9... | collective-permute-start | bytes 2359304 | tf_op jit(solution)/shard_map/while/body/eval_jaxpr/ppermute | solution.py:13
  386.3 17.5 %collective-permute-start.2 = (bf16[16,2,128,128]{3,2,1,0:T(8,128)(2,1)}, bf16[16,2,128,128]{3,2,1,0:T(8,128)(2,1)S(1)}, u32[]{:S(2)}, u32[]{:S(2)}) collective-permute-start(bf16[16,2,128,128]{3,2,1,0:T(8,128)(2,1)} %get-tuple-element.216), channel_id=1, source_target_pairs={{32,0},{64,32},{96,64},{128,96},{160,128},{192,160},{224,192},{256... | collective-permute-start | bytes 3145736 | tf_op jit(solution)/shard_map/while/body/eval_jaxpr/ppermute | solution.py:13
  421.0 16.3 %collective-permute-start.1 = (s32[3,24]{1,0:T(4,128)S(1)}, s32[3,24]{1,0:T(4,128)S(1)}, u32[]{:S(2)}, u32[]{:S(2)}) collective-permute-start(s32[3,24]{1,0:T(4,128)S(1)} %get-tuple-element.215), channel_id=1, source_target_pairs={{4,0},{8,4},{12,8},{16,12},{20,16},{24,20},{28,24},{0,28},{5,1},{9... | collective-permute-start | bytes 872 | tf_op jit(solution)/shard_map/while/body/eval_jaxpr/ppermute | solution.py:13
  423.8 13.4 %collective-permute-start.3 = (s32[16,2,2]{2,1,0:T(2,128)S(1)}, s32[16,2,2]{2,1,0:T(2,128)S(1)}, u32[]{:S(2)}, u32[]{:S(2)}) collective-permute-start(s32[16,2,2]{2,1,0:T(2,128)S(1)} %get-tuple-element.217), channel_id=1, source_target_pairs={{32,0},{64,32},{96,64},{128,96},{160,128},{192,160},{224,192},{256... | collective-permute-start | bytes 776 | tf_op jit(solution)/shard_map/while/body/eval_jaxpr/ppermute | solution.py:13
  429.1 15.4 %collective-permute-start = (bf16[24,128,128]{2,1,0:T(8,128)(2,1)}, bf16[24,128,128]{2,1,0:T(8,128)(2,1)}, u32[]{:S(2)}, u32[]{:S(2)}) collective-permute-start(bf16[24,128,128]{2,1,0:T(8,128)(2,1)} %get-tuple-element.214), channel_id=1, source_target_pairs={{4,0},{8,4},{12,8},{16,12},{20,16},{24,20},{28,24},{0,28},{5,1},{9... | collective-permute-start | bytes 2359304 | tf_op jit(solution)/shard_map/while/body/eval_jaxpr/ppermute | solution.py:13
  435.3 16.3 %collective-permute-start.2 = (bf16[16,2,128,128]{3,2,1,0:T(8,128)(2,1)}, bf16[16,2,128,128]{3,2,1,0:T(8,128)(2,1)S(1)}, u32[]{:S(2)}, u32[]{:S(2)}) collective-permute-start(bf16[16,2,128,128]{3,2,1,0:T(8,128)(2,1)} %get-tuple-element.216), channel_id=1, source_target_pairs={{32,0},{64,32},{96,64},{128,96},{160,128},{192,160},{224,192},{256... | collective-permute-start | bytes 3145736 | tf_op jit(solution)/shard_map/while/body/eval_jaxpr/ppermute | solution.py:13
  (6 other events, 90.9 us)
Sparse Core Ops, SparseCore 0:
  469.9 29.1 reduce-scatter.1
where the time goes:
time: 509 us; the launch traced here: 506 us
  waiting for transfers between devices  173 us (34%)
  starting transfers between devices  138 us (27%)
  local copies, waits for them, and re-layouts  85.1 us (17%)
  other arithmetic  64.2 us (13%)
  matrix products  30.6 us (6%)
  between operations  13.6 us (3%)
    ppermute x28, starting transfers between devices, passed_along(): return lax.ppermute(block, axis, route)  100 us
    ppermute x28, waiting for transfers between devices, passed_along(): return lax.ppermute(block, axis, route)  94.5 us
    scatter-add x8, other arithmetic, multiply(): running.at[target.reshape(-1)]  53.7 us
    dot_general x8, matrix products, multiply(): jnp.einsum('amn,awnp->awmp', a_held, picked, preferred_element_type=jnp.f...  30.6 us
    reduce_scatter x1, waiting for transfers between devices, shards(): lax.psum_scatter(running.astype(jnp.bfloat16), 'layer', scatter_dimension...  29.3 us
    reshape x8, local copies, waits for them, and re-layouts, multiply(): products.reshape(-1, a_held.shape[1], a_held.shape[2])  28.7 us
    while x28, local copies, waits for them, and re-layouts  21.7 us
    all_to_all x1, waiting for transfers between devices, shards(): lax.all_to_all(b_list, 'row', split_axis=0, concat_axis=0, tiled=True)  19.2 us
  transfers between devices with their start and end apart: 35, of which 20 were waited for; matrix products, arithmetic and copies ran while one was open for 9% of the time, Pallas kernels for 0%

commit v1 on v0

v1 whole, which is shorter than its diff:
```python
import functools

import jax
import jax.numpy as jnp
from jax import lax
from jax.experimental import pallas as pl
from jax.experimental.pallas import tpu as pltpu
from jax.sharding import PartitionSpec as P

BLOCK = 128
BATCH = 8
DEPTH = 8


def live_slots(send_list, live_count, slot_count):
    listed = lax.broadcasted_iota(jnp.int32, send_list.shape, 1) < live_count[:, None]
    slots = jnp.arange(slot_count, dtype=jnp.int32)
    return jnp.any((send_list[..., None] == slots) & listed[..., None], axis=(0, 1))


def product_list(a_code, b_code, c_index):
    c_rows, c_cols = c_index[0] // 16, c_index[1] // 8
    kept = c_rows.shape[0]
    a_inner, a_row = a_code // 32, a_code % 32
    b_inner, b_col = b_code // 64, b_code % 64
    slots = jnp.arange(kept, dtype=jnp.int32)
    slot = jnp.sum(
        jnp.where(
            (a_row[:, None, None] == c_rows) & (b_col[None, :, None] == c_cols), slots + 1, 0
        ),
        axis=2,
    )
    meets = (a_inner[:, None] == b_inner[None, :]) & (a_code >= 0)[:, None] & (slot > 0)
    position = jnp.arange(b_code.shape[0], dtype=jnp.int32)
    key = position[None, :] * 32 + slot - 1
    first = jnp.min(jnp.where(meets, key, 1 << 20), axis=1)
    last = jnp.max(jnp.where(meets, key, -1), axis=1)
    one = last >= 0
    two = one & (first != last)
    keys = jnp.concatenate([last, first])
    there = jnp.concatenate([one, two])
    a_slot = jnp.tile(jnp.arange(a_code.shape[0], dtype=jnp.int32), 2)
    total = keys.shape[0]
    entry = jnp.where(there, a_slot * 8192 + keys, 0)
    spots = jnp.arange(total, dtype=jnp.int32)
    rank = jnp.sum((there[None, :] & (spots[None, :] < spots[:, None])).astype(jnp.int32), axis=1)
    picked = there[:, None] & (rank[:, None] == spots[None, :])
    listed = jnp.sum(jnp.where(picked, entry[:, None], 0), axis=0)
    count = jnp.sum(there.astype(jnp.int32))
    return jnp.where(spots < count, listed, kept), count[None]


def product_kernel(
    list_ref, count_ref, a_ref, b_ref, out_ref, a_buffer, b_buffer, total, a_sem, b_sem
):
    kept = out_ref.shape[0]
    batches = (count_ref[0] + BATCH - 1) // BATCH

    def fetch(batch):
        spot = batch % DEPTH
        for n in range(BATCH):
            entry = list_ref[batch * BATCH + n]
            pltpu.make_async_copy(
                a_ref.at[entry // 8192], a_buffer.at[spot, n], a_sem.at[spot]
            ).start()
            pltpu.make_async_copy(
                b_ref.at[(entry // 32) % 256], b_buffer.at[spot, n], b_sem.at[spot]
            ).start()

    def prefetch(batch, carry):
        fetch(batch)
        return carry

    lax.fori_loop(0, jnp.minimum(batches, DEPTH), prefetch, 0)
    total[...] = jnp.zeros_like(total)

    def work(batch, carry):
        spot = batch % DEPTH
        pltpu.make_async_copy(a_buffer.at[spot], a_buffer.at[spot], a_sem.at[spot]).wait()
        pltpu.make_async_copy(b_buffer.at[spot], b_buffer.at[spot], b_sem.at[spot]).wait()
        products = [
            jnp.dot(
                a_buffer[spot, n], b_buffer[spot, n], preferred_element_type=jnp.float32
            )
            for n in range(BATCH)
        ]
        for n in range(BATCH):
            slot = list_ref[batch * BATCH + n] % 32
            total[slot] += products[n]

        @pl.when(batch + DEPTH < batches)
        def _():
            fetch(batch + DEPTH)

        return carry

    lax.fori_loop(0, batches, work, 0)
    out_ref[...] = total[0:kept].astype(out_ref.dtype)


def partial_product(listed, count, a_all, b_all, kept):
    smem = pl.BlockSpec(memory_space=pltpu.SMEM)
    anywhere = pl.BlockSpec(memory_space=pl.ANY)
    return pl.pallas_call(
        product_kernel,
        out_shape=jax.ShapeDtypeStruct((kept, BLOCK, BLOCK), jnp.bfloat16),
        in_specs=[smem, smem, anywhere, anywhere],
        out_specs=pl.BlockSpec(memory_space=pltpu.VMEM),
        scratch_shapes=[
            pltpu.VMEM((DEPTH, BATCH, BLOCK, BLOCK), jnp.bfloat16),
            pltpu.VMEM((DEPTH, BATCH, BLOCK, BLOCK), jnp.bfloat16),
            pltpu.VMEM((kept + 1, BLOCK, BLOCK), jnp.float32),
            pltpu.SemaphoreType.DMA((DEPTH,)),
            pltpu.SemaphoreType.DMA((DEPTH,)),
        ],
        compiler_params=pltpu.CompilerParams(vmem_limit_bytes=32 << 20),
        name="partial_product",
    )(listed, count, a_all, b_all)


def shards(a_blocks, a_index, a_send, a_count, b_blocks, b_index, b_send, b_count, c_index):
    a_own, b_own = a_blocks[0, 0, 0], b_blocks[0, 0, 0]
    a_rows, a_cols = a_index[0, 0, 0, 0], a_index[0, 0, 0, 1]
    b_rows, b_cols = b_index[0, 0, 0, 0], b_index[0, 0, 0, 1]
    a_live = live_slots(a_send[0, 0, 0], a_count[0, 0, 0], a_own.shape[0])
    b_live = live_slots(b_send[0, 0, 0], b_count[0, 0, 0], b_own.shape[0])
    a_code = jnp.where(a_live, (a_cols // 32 * 8 + a_cols % 8) * 32 + a_rows // 16, -1)
    b_code = jnp.where(b_live, (b_rows // 32 * 8 + b_rows % 8) * 64 + b_cols // 8, -1)
    a_code = lax.all_gather(a_code, "col", tiled=True)
    b_code = lax.all_gather(b_code, "row", tiled=True)
    a_all = lax.all_gather(a_own, "col", tiled=True)
    b_all = lax.all_gather(b_own, "row", tiled=True)
    listed, count = product_list(a_code, b_code, c_index[0, 0])
    partial = partial_product(listed, count, a_all, b_all, c_index.shape[3])
    result = lax.psum_scatter(partial, "layer", scatter_dimension=0, tiled=True)
    return result[None, None]


def solution(mesh):
    in_specs = (
        P("row", "col", "layer", None, None, None),
        P("row", "col", "layer", None, None),
        P("row", "col", "layer", None, None),
        P("row", "col", "layer", None),
        P("row", "col", "layer", None, None, None),
        P("row", "col", "layer", None, None),
        P("row", "col", "layer", None, None),
        P("row", "col", "layer", None),
        P("row", "col", None, None),
    )
    out_specs = P("row", "col", "layer", None, None)
    return jax.shard_map(shards, mesh=mesh, in_specs=in_specs, out_specs=out_specs, check_vma=False)
```

time: 509 us -> 283 us (0.56)
  starting transfers between devices: 138 us -> 0.08 us
  local copies, waits for them, and re-layouts: 85.1 us -> 9.53 us
  other arithmetic: 64.2 us -> 8.82 us
  waiting for transfers between devices: 173 us -> 208 us
  blocking collectives: 0 us -> 32.5 us
  matrix products: 30.6 us -> 0 us
  Pallas kernels: 0 us -> 8.82 us
    all_gather x0 -> x2, waiting for transfers between devices: none -> 180 us  [the longest x1 142 us: shards(): b_all = lax.all_gather(b_own, 'row', tiled=True)]
    ppermute x28 -> x0, starting transfers between devices: 100 us -> none  [passed_along(): return lax.ppermute(block, axis, route)]
    ppermute x28 -> x0, waiting for transfers between devices: 94.5 us -> none  [passed_along(): return lax.ppermute(block, axis, route)]
    scatter-add x8 -> x0, other arithmetic: 53.7 us -> none  [multiply(): running.at[target.reshape(-1)]]
    all_to_all x6 -> x0, waiting for transfers between devices: 49.3 us -> none  [the longest x1 19.2 us: shards(): lax.all_to_all(b_list, 'row', split_axis=0, concat_axis=0, tiled=True)]
    all_to_all x6 -> x0, starting transfers between devices: 38.3 us -> none  [the longest x1 10.9 us: shards(): lax.all_to_all(a_live, 'col', split_axis=0, concat_axis=0, tiled=True)]
    unnamed x0 -> x2, blocking collectives: none -> 32.5 us
    dot_general x8 -> x0, matrix products: 30.6 us -> none  [multiply(): jnp.einsum('amn,awnp->awmp', a_held, picked, preferred_element_type=jnp.f...]
  transfers between devices with their start and end apart: 35 -> 3, of which waited for: 20 -> 3; matrix products, arithmetic and copies ran while one was open for 9% -> 4% of each run, Pallas kernels for 0% -> 0%
where the time goes in v1:
time: 283 us
  waiting for transfers between devices  208 us (73%)
  blocking collectives  32.5 us (11%)
  between operations  14.5 us (5%)
  local copies, waits for them, and re-layouts  9.53 us (3%)
  other arithmetic  8.82 us (3%)
  Pallas kernels  8.82 us (3%)
    all_gather x1, waiting for transfers between devices, shards(): b_all = lax.all_gather(b_own, 'row', tiled=True)  142 us
    all_gather x1, waiting for transfers between devices, shards(): a_all = lax.all_gather(a_own, 'col', tiled=True)  38.8 us
    unnamed x2, blocking collectives  32.5 us
    reduce_scatter x1, waiting for transfers between devices, shards(): result = lax.psum_scatter(partial, 'layer', scatter_dimension=0, tiled=True)  26.5 us
    unnamed x9, local copies, waits for them, and re-layouts  9.45 us
    pallas_call x1, Pallas kernels, partial_product(): pl.pallas_call(product_kernel, out_shape=jax.ShapeDtypeStruct((kept, BLOC...  8.82 us
  transfers between devices with their start and end apart: 3, of which 3 were waited for; matrix products, arithmetic and copies ran while one was open for 4% of the time, Pallas kernels for 0%

profile of v1, /device:TPU:1, one launch (start us, length us, event | category | flops | bytes accessed | tf_op | source)
XLA Modules:
  0.0 282.6 jit_solution(16974584228200709074)
XLA Ops:
  6.5 0.7 all-gather.5.cloned.1.call-update
  7.3 0.0 all-gather.7.cloned.1.call-start
  7.3 0.7 all-gather.7.cloned.1.call-update
  8.0 0.0 reduce-scatter.2.cloned.1.call-start
  8.1 1.3 dynamic-slice.1
  9.3 1.3 dynamic-slice
  10.7 0.7 copy.20
  11.3 0.1 mul.44
  12.7 0.7 iota_compare_fusion.4
  13.4 0.1 fusion.5
  13.5 0.9 select_dynamic-update-slice_fusion.1
  14.3 16.8 %all-reduce = s32[192]{0:T(256)S(1)} all-reduce(s32[192]{0:T(256)S(1)} %select_dynamic-update-slice_fusion.1), channel_id=1, replica_groups=mesh['row'=16,'col'=8,'layer'=4] {'col'}, use_global_device_ids=true, to_apply=%add | all-reduce | flops 192 | bytes 1536
  31.1 0.7 iota_compare_fusion.6
  31.8 0.8 fusion.3
  32.5 0.9 select_dynamic-update-slice_fusion
  33.4 15.8 %all-reduce.1 = s32[256]{0:T(256)S(1)} all-reduce(s32[256]{0:T(256)S(1)} %select_dynamic-update-slice_fusion), channel_id=1, replica_groups=mesh['row'=16,'col'=8,'layer'=4] {'row'}, use_global_device_ids=true, to_apply=%add.1 | all-reduce | flops 256 | bytes 2048
  49.2 0.8 and_select_fusion.2
  50.0 0.1 broadcast_compare_fusion.1
  50.1 0.1 broadcast_compare_fusion
  50.2 1.8 select_reduce_fusion
  52.0 0.3 select_reduce_fusion.3
  52.3 0.7 convert_reduce_fusion.1
  53.0 0.1 convert_reduce_fusion
  53.2 0.1 fusion.6
  53.2 0.2 select_reduce_fusion.1
  53.5 0.7 fusion.7.list_ref
  54.1 38.8 %all-gather.5.cloned.1.call-done = bf16[1,1,1,192,128,128]{5,4,2,1,0,3:T(8,128)(2,1)} async-done(((bf16[1,1,1,24,128,128]{5,4,2,1,0,3:T(8,128)(2,1)}), bf16[1,1,1,192,128,128]{5,4,2,1,0,3:T(8,128)(2,1)}) %all-gather.5.cloned.1.call-update) | async-done | bytes 6291472 | tf_op jit(solution)/shard_map/all_gather | solution.py:131
  92.9 141.7 %all-gather.7.cloned.1.call-done = bf16[1,1,1,256,128,128]{5,4,2,1,0,3:T(8,128)(2,1)} async-done(((bf16[1,1,1,16,128,128]{5,4,2,1,0,3:T(8,128)(2,1)}), bf16[1,1,1,256,128,128]{5,4,2,1,0,3:T(8,128)(2,1)}) %all-gather.7.cloned.1.call-update) | async-done | bytes 8388624 | tf_op jit(solution)/shard_map/all_gather | solution.py:132
  234.6 3.4 %copy-done = bf16[1,1,1,256,128,128]{5,4,2,1,0,3:T(8,128)(2,1)S(1)} copy-done((bf16[1,1,1,256,128,128]{5,4,2,1,0,3:T(8,128)(2,1)S(1)}, bf16[1,1,1,256,128,128]{5,4,2,1,0,3:T(8,128)(2,1)}, u32[]{:S(2)}) %copy-start) | copy-done | bytes 8388632
  238.0 2.8 copy-done.1
  240.7 8.8 %partial_product.1 = bf16[24,128,128]{2,1,0:T(8,128)(2,1)} custom-call(s32[384]{0:T(512)S(1)} %fusion.7.list_ref, s32[1]{0:T(128)} %bitcast.11.count_ref, bf16[192,128,128]{2,1,0:T(8,128)(2,1)S(1)} %bitcast.77, bf16[256,128,128]{2,1,0:T(8,128)(2,1)S(1)} %bitcast.76), custom_call_target="tpu_custom_call" | custom-call | tf_op jit(solution)/shard_map/partial_product/pallas_call | solution.py:104
  249.6 26.5 %reduce-scatter.2.cloned.1.call-done = bf16[6,128,128]{2,1,0:T(8,128)(2,1)} async-done(((bf16[24,128,128]{2,1,0:T(8,128)(2,1)}), bf16[6,128,128]{2,1,0:T(8,128)(2,1)}) %reduce-scatter.2.cloned.1.call-update) | async-done | bytes 196624 | tf_op jit(solution)/shard_map/reduce_scatter | solution.py:135
  (13 shorter events, 0.1 us)
Async XLA Ops:
  6.5 86.4 %all-gather.5.cloned.1.call-start = ((), (), s32[]{:S(2)}) async-start(), calls=%async_computation.2 | async-start | bytes 7077888 | tf_op jit(solution)/shard_map/all_gather | solution.py:131
  7.3 227.3 %all-gather.7.cloned.1.call-start = ((), (), s32[]{:S(2)}) async-start(), calls=%async_computation.3 | async-start | bytes 8912896 | tf_op jit(solution)/shard_map/all_gather | solution.py:132
  8.0 268.1 %reduce-scatter.2.cloned.1.call-start = ((), (), s32[]{:S(2)}) async-start(), calls=%async_computation.1 | async-start | bytes 983040 | tf_op jit(solution)/shard_map/reduce_scatter | solution.py:135
  234.6 3.4 %copy-start = (bf16[1,1,1,256,128,128]{5,4,2,1,0,3:T(8,128)(2,1)S(1)}, bf16[1,1,1,256,128,128]{5,4,2,1,0,3:T(8,128)(2,1)}, u32[]{:S(2)}) copy-start(bf16[1,1,1,256,128,128]{5,4,2,1,0,3:T(8,128)(2,1)} %all-gather.7.cloned.1.call-done) | copy-start | bytes 25165828
  238.0 2.8 copy-start.1
Sparse Core Ops, SparseCore 0:
  9.4 83.4 all-gather.4
  96.1 138.4 all-gather.6
  249.7 26.3 reduce-scatter.1

commit v2 on v1

--- a/solution.py
+++ b/solution.py
@@ -10,6 +10,8 @@
 BLOCK = 128
 BATCH = 8
 DEPTH = 8
+SEMAPHORES = 128
+MESH = pl.DeviceIdType.MESH
 
 
 def live_slots(send_list, live_count, slot_count):
@@ -113,9 +115,283 @@
             pltpu.SemaphoreType.DMA((DEPTH,)),
             pltpu.SemaphoreType.DMA((DEPTH,)),
         ],
-        compiler_params=pltpu.CompilerParams(vmem_limit_bytes=32 << 20),
+        compiler_params=pltpu.CompilerParams(vmem_limit_bytes=60 << 20),
         name="partial_product",
     )(listed, count, a_all, b_all)
+
+
+A_CHUNKS = ((0, 6, 1), (6, 6, 1), (12, 6, -1), (18, 6, -1))
+B_CHUNKS = ((0, 4, 1, True), (4, 4, -1, True), (8, 4, 1, False), (12, 4, -1, False))
+
+
+def gather_kernel(a_ref, b_ref, m_ref, a_all, b_all, a_marks, b_marks, send_sem, recv_sem, own_sem):
+    col, row = lax.axis_index("col"), lax.axis_index("row")
+    a_ring, b_ring = lax.axis_size("col"), lax.axis_size("row") // 2
+    plane, spot = row // b_ring, row % b_ring
+    partner = row + b_ring - 2 * b_ring * plane
+
+    def a_peer(way):
+        return {"col": lax.rem(col + way + a_ring, a_ring)}
+
+    def b_peer(way):
+        return {"row": plane * b_ring + lax.rem(spot + way + b_ring, b_ring)}
+
+    barrier = pltpu.get_barrier_semaphore()
+    peers = (a_peer(1), a_peer(-1), b_peer(1), b_peer(-1), {"row": partner})
+    for peer in peers:
+        pl.semaphore_signal(barrier, inc=1, device_id=peer, device_id_type=MESH)
+    pl.semaphore_wait(barrier, len(peers))
+
+    numbers = {}
+    sent = []
+
+    def number(name):
+        return numbers.setdefault(name, len(numbers))
+
+    def send(name, source, target, peer):
+        at = number(name)
+        copy = pltpu.make_async_remote_copy(
+            src_ref=source,
+            dst_ref=target,
+            send_sem=send_sem.at[at],
+            recv_sem=recv_sem.at[at],
+            device_id=peer,
+            device_id_type=MESH,
+        )
+        copy.start()
+        sent.append(copy)
+
+    def arrive(name, target, peer):
+        at = number(name)
+        pltpu.make_async_remote_copy(
+            src_ref=target,
+            dst_ref=target,
+            send_sem=send_sem.at[at],
+            recv_sem=recv_sem.at[at],
+            device_id=peer,
+            device_id_type=MESH,
+        ).wait_recv()
+
+    a_pieces = [("marks", lambda o: a_marks.at[o], m_ref, 1, 0.0)]
+    for n, (start, size, way) in enumerate(A_CHUNKS):
+        a_pieces.append(
+            (
+                f"a{n}",
+                lambda o, start=start, size=size: a_all.at[o, pl.ds(start, size)],
+                a_ref.at[pl.ds(start, size)],
+                way,
+                size,
+            )
+        )
+    b_pieces = [("marks", lambda o: b_marks.at[o], m_ref, 1, 0.0, False)]
+    for n, (start, size, way, later) in enumerate(B_CHUNKS):
+        b_pieces.append(
+            (
+                f"b{n}",
+                lambda o, start=start, size=size: b_all.at[o, pl.ds(start, size)],
+                b_ref.at[pl.ds(start, size)],
+                way,
+                size,
+                later,
+            )
+        )
+
+    events = []
+
+    def forward_a(piece, way, step, origin, source):
+        last = a_ring // 2
+        if step < last or (step == last and piece[3] == way):
+            send(("a", piece[0], way, step), source, piece[1](origin), a_peer(way))
+
+    def forward_b(piece, way, step, side, origin, source):
+        last = b_ring // 2
+        if step < last or (step == last and piece[3] == way):
+            send(("b", piece[0], way, step, side), source, piece[1](origin), b_peer(way))
+
+    def b_origin(side, place):
+        return (plane if side == "own" else 1 - plane) * b_ring + place
+
+    for piece in b_pieces:
+        if not piece[5]:
+            send(("x", piece[0], 0, 0), piece[2], piece[1](row), {"row": partner})
+    own = [
+        pltpu.make_async_copy(a_ref, a_all.at[col], own_sem.at[0]),
+        pltpu.make_async_copy(b_ref, b_all.at[row], own_sem.at[1]),
+        pltpu.make_async_copy(m_ref, a_marks.at[col], own_sem.at[2]),
+        pltpu.make_async_copy(m_ref, b_marks.at[row], own_sem.at[3]),
+    ]
+    for way in (1, -1):
+        forward_a(a_pieces[0], way, 1, col, a_pieces[0][2])
+        forward_b(b_pieces[0], way, 1, "own", row, b_pieces[0][2])
+    for rank in range(len(A_CHUNKS)):
+        for way in (1, -1):
+            piece = a_pieces[1:][rank if way == 1 else -1 - rank]
+            forward_a(piece, way, 1, col, piece[2])
+    for rank in range(len(B_CHUNKS)):
+        for way in (1, -1):
+            piece = b_pieces[1:][rank if way == 1 else -1 - rank]
+            forward_b(piece, way, 1, "own", row, piece[2])
+    for piece in b_pieces:
+        if piece[5]:
+            send(("x", piece[0], 0, 0), piece[2], piece[1](row), {"row": partner})
+    for copy in own:
+        copy.start()
+
+    a_step = sum(piece[4] for piece in a_pieces)
+    b_step = sum(piece[4] * (1 if piece[5] else 2) for piece in b_pieces)
+
+    def arrive_a(piece, way, step):
+        origin = lax.rem(col - way * step + a_ring, a_ring)
+        place = piece[1](origin)
+        arrive(("a", piece[0], way, step), place, a_peer(way))
+        forward_a(piece, way, step + 1, origin, place)
+
+    def arrive_b(piece, way, step, side):
+        origin = b_origin(side, lax.rem(spot - way * step + b_ring, b_ring))
+        place = piece[1](origin)
+        arrive(("b", piece[0], way, step, side), place, b_peer(way))
+        forward_b(piece, way, step + 1, side, origin, place)
+        if piece[5]:
+            send(("x", piece[0], way, step), place, place, {"row": partner})
+
+    def arrive_x(piece, way, step):
+        origin = b_origin("far", lax.rem(spot - way * step + b_ring, b_ring))
+        place = piece[1](origin)
+        arrive(("x", piece[0], way, step), place, {"row": partner})
+        if step == 0 and not piece[5]:
+            for on in (1, -1):
+                forward_b(piece, on, 1, "far", origin, place)
+
+    for way in (1, -1):
+        for step in range(1, a_ring // 2 + 1):
+            done = (step - 1) * a_step
+            for piece in a_pieces[:1] + a_pieces[1:][::way]:
+                if step < a_ring // 2 or piece[3] == way:
+                    done += piece[4]
+                    events.append((2 * done, functools.partial(arrive_a, piece, way, step)))
+        for step in range(1, b_ring // 2 + 1):
+            done = (step - 1) * b_step
+            for side in ("own", "far"):
+                for piece in b_pieces[:1] + b_pieces[1:][::way]:
+                    if side == "far" and piece[5]:
+                        continue
+                    if step < b_ring // 2 or piece[3] == way:
+                        done += piece[4]
+                        events.append(
+                            (2 * done, functools.partial(arrive_b, piece, way, step, side))
+                        )
+                        if piece[5]:
+                            events.append(
+                                (2 * done + 40, functools.partial(arrive_x, piece, way, step))
+                            )
+    x_done = 0
+    for piece in b_pieces:
+        if not piece[5]:
+            x_done += piece[4]
+            events.append((3 * x_done, functools.partial(arrive_x, piece, 0, 0)))
+    for piece in b_pieces:
+        if piece[5]:
+            events.append((60, functools.partial(arrive_x, piece, 0, 0)))
+    for _, event in sorted(events, key=lambda e: e[0]):
+        event()
+    for copy in own:
+        copy.wait()
+    for copy in sent:
+        copy.wait_send()
+    assert len(numbers) <= SEMAPHORES
+
+
+def gathered(a_own, b_own, marks):
+    anywhere = pl.BlockSpec(memory_space=pl.ANY)
+    cols, rows = lax.axis_size("col"), lax.axis_size("row")
+    return pl.pallas_call(
+        gather_kernel,
+        out_shape=(
+            jax.ShapeDtypeStruct((cols,) + a_own.shape, a_own.dtype),
+            jax.ShapeDtypeStruct((rows,) + b_own.shape, b_own.dtype),
+            jax.ShapeDtypeStruct((cols,) + marks.shape, marks.dtype),
+            jax.ShapeDtypeStruct((rows,) + marks.shape, marks.dtype),
+        ),
+        in_specs=[anywhere] * 3,
+        out_specs=(anywhere,) * 4,
+        scratch_shapes=[
+            pltpu.SemaphoreType.DMA((SEMAPHORES,)),
+            pltpu.SemaphoreType.DMA((SEMAPHORES,)),
+            pltpu.SemaphoreType.DMA((4,)),
+        ],
+        compiler_params=pltpu.CompilerParams(
+            collective_id=0, has_side_effects=True, vmem_limit_bytes=60 << 20
+        ),
+        name="gather_blocks",
+    )(a_own, b_own, marks)
+
+
+def layer_sum_kernel(partial_ref, out_ref, from_sibling, pair, from_far, send_sem, recv_sem):
+    layer = lax.axis_index("layer")
+    share = out_ref.shape[0]
+    sibling = {"layer": layer + 1 - 2 * lax.rem(layer, 2)}
+    far = {"layer": lax.rem(layer + 2, 4)}
+    barrier = pltpu.get_barrier_semaphore()
+    for peer in (sibling, far):
+        pl.semaphore_signal(barrier, inc=1, device_id=peer, device_id_type=MESH)
+    pl.semaphore_wait(barrier, 2)
+
+    def group(ref, owner):
+        return ref.at[pl.ds(owner * share, share)]
+
+    def copy(n, source, target, peer):
+        return pltpu.make_async_remote_copy(
+            src_ref=source,
+            dst_ref=target,
+            send_sem=send_sem.at[n],
+            recv_sem=recv_sem.at[n],
+            device_id=peer,
+            device_id_type=MESH,
+        )
+
+    on = copy(0, group(partial_ref, lax.rem(sibling["layer"] + 2, 4)), from_sibling.at[0], sibling)
+    kept = copy(1, group(partial_ref, sibling["layer"]), from_sibling.at[1], sibling)
+    on.start()
+    kept.start()
+    on.wait_recv()
+    pair[...] = (
+        group(partial_ref, far["layer"])[...].astype(jnp.float32)
+        + from_sibling[0].astype(jnp.float32)
+    ).astype(pair.dtype)
+    across = copy(2, pair, from_far, far)
+    across.start()
+    kept.wait_recv()
+    across.wait_recv()
+    out_ref[...] = (
+        group(partial_ref, layer)[...].astype(jnp.float32)
+        + from_sibling[1].astype(jnp.float32)
+        + from_far[...].astype(jnp.float32)
+    ).astype(out_ref.dtype)
+    on.wait_send()
+    kept.wait_send()
+    across.wait_send()
+
+
+def layer_sum(partial):
+    share = (partial.shape[0] // lax.axis_size("layer"),) + partial.shape[1:]
+    vmem = pl.BlockSpec(memory_space=pltpu.VMEM)
+    return pl.pallas_call(
+        layer_sum_kernel,
+        out_shape=jax.ShapeDtypeStruct(share, partial.dtype),
+        in_specs=[vmem],
+        out_specs=vmem,
+        scratch_shapes=[
+            pltpu.VMEM((2,) + share, partial.dtype),
+            pltpu.VMEM(share, partial.dtype),
+            pltpu.VMEM(share, partial.dtype),
+            pltpu.SemaphoreType.DMA((3,)),
+            pltpu.SemaphoreType.DMA((3,)),
+        ],
+        compiler_params=pltpu.CompilerParams(
+            collective_id=1, has_side_effects=True, vmem_limit_bytes=60 << 20
+        ),
+        name="layer_sum",
+    )(partial)
 
 
 def shards(a_blocks, a_index, a_send, a_count, b_blocks, b_index, b_send, b_count, c_index):
@@ -126,14 +402,17 @@
     b_live = live_slots(b_send[0, 0, 0], b_count[0, 0, 0], b_own.shape[0])
     a_code = jnp.where(a_live, (a_cols // 32 * 8 + a_cols % 8) * 32 + a_rows // 16, -1)
     b_code = jnp.where(b_live, (b_rows // 32 * 8 + b_rows % 8) * 64 + b_cols // 8, -1)
-    a_code = lax.all_gather(a_code, "col", tiled=True)
-    b_code = lax.all_gather(b_code, "row", tiled=True)
-    a_all = lax.all_gather(a_own, "col", tiled=True)
-    b_all = lax.all_gather(b_own, "row", tiled=True)
+    codes = jnp.concatenate([a_code, b_code, jnp.full((88,), -1, jnp.int32)])
+    marks = jnp.broadcast_to(codes, (8, 128))
+    a_all, b_all, a_marks, b_marks = gathered(a_own, b_own, marks)
+    a_held, b_held = a_own.shape[0], b_own.shape[0]
+    a_code = a_marks[:, 0, :a_held].reshape(-1)
+    b_code = b_marks[:, 0, a_held : a_held + b_held].reshape(-1)
+    a_all = a_all.reshape(-1, BLOCK, BLOCK)
+    b_all = b_all.reshape(-1, BLOCK, BLOCK)
     listed, count = product_list(a_code, b_code, c_index[0, 0])
     partial = partial_product(listed, count, a_all, b_all, c_index.shape[3])
-    result = lax.psum_scatter(partial, "layer", scatter_dimension=0, tiled=True)
-    return result[None, None]
+    return layer_sum(partial)[None, None]
 
 
 def solution(mesh):

time: 283 us -> 113 us (0.40)
  waiting for transfers between devices: 208 us -> 0 us
  Pallas kernels: 8.82 us -> 98.4 us
  blocking collectives: 32.5 us -> 0 us
  between operations: 14.5 us -> 0.09 us
  local copies, waits for them, and re-layouts: 9.53 us -> 4.85 us
    all_gather x2 -> x0, waiting for transfers between devices: 180 us -> none  [the longest x1 142 us: shards(): b_all = lax.all_gather(b_own, 'row', tiled=True)]
    pallas_call x0 -> x2, Pallas kernels: none -> 93.2 us  [the longest x1 80.4 us: gathered(): pl.pallas_call(gather_kernel, out_shape=(jax.ShapeDtypeStruct((cols,) + a...]
    unnamed x2 -> x0, blocking collectives: 32.5 us -> none
    reduce_scatter x1 -> x0, waiting for transfers between devices: 26.5 us -> none  [shards(): result = lax.psum_scatter(partial, 'layer', scatter_dimension=0, tiled=True)]
    unnamed x9 -> x2, local copies, waits for them, and re-layouts: 9.45 us -> 2.3 us
    pallas_call x1, Pallas kernels: 8.82 us -> 5.2 us  [partial_product(): pl.pallas_call(product_kernel, out_shape=jax.ShapeDtypeStruct((kept, BLOC...]
  transfers between devices with their start and end apart: 3 -> 0, of which waited for: 3 -> 0; matrix products, arithmetic and copies ran while one was open for 4% -> 0% of each run, Pallas kernels for 0% -> 0%
where the time goes in v2:
time: 113 us
  Pallas kernels  98.4 us (87%)
  other arithmetic  9.22 us (8%)
  local copies, waits for them, and re-layouts  4.85 us (4%)
    pallas_call x1, Pallas kernels, gathered(): pl.pallas_call(gather_kernel, out_shape=(jax.ShapeDtypeStruct((cols,) + a...  80.4 us
    pallas_call x1, Pallas kernels, layer_sum(): pl.pallas_call(layer_sum_kernel, out_shape=jax.ShapeDtypeStruct(share, pa...  12.8 us
    pallas_call x1, Pallas kernels, partial_product(): pl.pallas_call(product_kernel, out_shape=jax.ShapeDtypeStruct((kept, BLOC...  5.2 us
    unnamed x2, local copies, waits for them, and re-layouts  2.3 us

profile of v2, /device:TPU:1, one launch (start us, length us, event | category | flops | bytes accessed | tf_op | source)
XLA Modules:
  0.0 112.6 jit_solution(11833910263088231934)
XLA Ops:
  0.0 0.7 iota_compare_fusion.4
  0.7 0.7 iota_compare_fusion.6
  1.3 0.8 fusion.3
  2.1 0.8 add_select_fusion
  2.9 0.8 and_select_fusion.2
  3.6 0.7 copy.14
  4.3 0.1 fusion.5
  4.4 0.8 add_select_fusion.1
  5.2 0.1 pad_add_fusion.1
  5.3 0.1 mul.44
  5.4 0.6 broadcast_in_dim.68.m_ref
  6.0 80.4 %gather_blocks.1 = (bf16[8,24,128,128]{3,2,1,0:T(8,128)(2,1)}, bf16[16,16,128,128]{3,2,1,0:T(8,128)(2,1)}, s32[8,8,128]{2,1,0:T(8,128)}, s32[16,8,128]{2,1,0:T(8,128)}) custom-call(bf16[24,128,128]{2,1,0:T(8,128)(2,1)} %bitcast.76, bf16[16,128,128]{2,1,0:T(8,128)(2,1)} %bitcast.78, s32[8,128]{1,0:T(8,128)} %broadcast_in_dim.68.m_ref), custom_call_target="tpu_custom_call" | custom-call | tf_op jit(solution)/shard_map/gather_blocks/pallas_call | solution.py:307
  86.4 0.8 slice_reduce_fusion.1
  87.2 0.1 reshape_squeeze.6
  87.3 0.9 slice_reduce_fusion
  88.2 0.1 reshape_squeeze.7
  88.3 0.1 broadcast_compare_fusion.1
  88.4 0.1 broadcast_compare_fusion
  88.5 1.8 %select_reduce_fusion = s32[192,256]{1,0:T(8,128)S(1)} fusion(s32[24]{0:T(128)S(1)} %iota_add_fusion, pred[256,24]{0,1:T(8,128)(4,1)S(1)} %broadcast_compare_fusion.1, pred[192,24]{1,0:T(8,128)(4,1)S(1)} %broadcast_compare_fusion), kind=kLoop, calls=%fused_computation | loop fusion | flops 3489792 | bytes 207456 | tf_op jit(solution)/shard_map/reduce_sum | solution.py:29
  90.3 0.3 select_reduce_fusion.3
  90.6 0.7 convert_reduce_fusion.1
  91.3 0.1 fusion.6
  91.4 0.1 convert_reduce_fusion
  91.6 0.2 select_reduce_fusion.1
  91.8 1.2 %fusion.7.list_ref = s32[384]{0:T(512)} fusion(s32[384]{0:T(512)S(1)} %select_reduce_fusion.1, s32[]{:T(128)} %get-tuple-element.15), kind=kLoop, calls=%fused_computation.28 | loop fusion | flops 768 | bytes 3076 | tf_op jit(solution)/shard_map/jit(_where)/select_n | solution.py:52
  93.0 5.2 %partial_product.1.partial_ref = bf16[24,128,128]{2,1,0:T(8,128)(2,1)} custom-call(s32[384]{0:T(512)} %fusion.7.list_ref, s32[1]{0:T(128)} %bitcast.11.count_ref, bf16[192,128,128]{2,1,0:T(8,128)(2,1)} %bitcast.75, bf16[256,128,128]{2,1,0:T(8,128)(2,1)} %bitcast.74), custom_call_target="tpu_custom_call" | custom-call | tf_op jit(solution)/shard_map/partial_product/pallas_call | solution.py:106
  98.2 12.8 %layer_sum.1 = bf16[6,128,128]{2,1,0:T(8,128)(2,1)} custom-call(bf16[24,128,128]{2,1,0:T(8,128)(2,1)} %partial_product.1.partial_ref), custom_call_target="tpu_custom_call" | custom-call | tf_op jit(solution)/shard_map/layer_sum/pallas_call | solution.py:378
  111.0 1.6 %copy.16 = bf16[1,1,6,128,128]{4,3,2,1,0:T(8,128)(2,1)} copy(bf16[1,1,6,128,128]{4,3,2,1,0:T(8,128)(2,1)} %bitcast.77) | data formatting | bytes 393216
  (7 shorter events, 0.1 us)

commit v3 on v2

v3 whole, which is shorter than its diff:
```python
import functools

import jax
import jax.numpy as jnp
from jax import lax
from jax.experimental import pallas as pl
from jax.experimental.pallas import tpu as pltpu
from jax.sharding import PartitionSpec as P

BLOCK = 128
BATCH = 8
DEPTH = 4
SEMAPHORES = 128
PIECES = 3
MESH = pl.DeviceIdType.MESH


def own_marks(col, row, a_index, a_send, a_count, b_index, b_send, b_count):
    shape = (8, 128)
    place = lax.broadcasted_iota(jnp.int32, shape, 0) * 128 + lax.broadcasted_iota(
        jnp.int32, shape, 1
    )
    marks = jnp.zeros(shape, jnp.int32)
    for base, first, index, inner_at, send, count in (
        (0, col * a_index.shape[4], a_index, 1, a_send, a_count),
        (512, row * b_index.shape[4], b_index, 0, b_send, b_count),
    ):
        spread = 16 if inner_at else 8
        live = place < 0
        for d in range(send.shape[1]):
            for m in range(send.shape[0]):
                slot = jnp.where(m < count[0, 0, 0, d], base + first + send[m, d], -1)
                live = live | (place == slot)
        inner = jnp.zeros(shape, jnp.int32)
        for slot in range(index.shape[4]):
            k = index[0, 0, 0, inner_at, slot]
            other = index[0, 0, 0, 1 - inner_at, slot]
            inner = jnp.where(
                place == base + first + slot, lax.div(k, 32) * 8 + lax.rem(k, 8) + 1, inner
            )
            marks = jnp.where(place == base + 256 + first + slot, lax.div(other, spread), marks)
        marks = jnp.where(live, inner, marks)
    return marks


def product_list(a_marks, b_marks, c_index):
    kept = c_index.shape[3]
    a_sum = a_marks[0]
    for n in range(1, a_marks.shape[0]):
        a_sum = a_sum + a_marks[n]
    b_sum = b_marks[0]
    for n in range(1, b_marks.shape[0]):
        b_sum = b_sum + b_marks[n]
    square = (128, 128)
    sub = lax.broadcasted_iota(jnp.int32, square, 0)
    lane = lax.broadcasted_iota(jnp.int32, square, 1)
    sub_f, lane_f = sub.astype(jnp.float32), lane.astype(jnp.float32)
    eye = sub == lane

    def column(values):
        return jnp.sum(jnp.where(eye, values, 0.0), axis=1, keepdims=True)

    def line(values):
        return jnp.sum(jnp.where(eye, values, 0.0), axis=0, keepdims=True)

    a_f, b_f = a_sum.astype(jnp.float32), b_sum.astype(jnp.float32)
    c_code = [
        (lax.div(c_index[0, 0, 0, m], 16) * 64 + lax.div(c_index[0, 0, 1, m], 8)).astype(
            jnp.float32
        )
        for m in range(kept)
    ]
    entries = []
    for i in range(2):
        a_inner = column(a_f[i : i + 1])
        a_row = column(a_f[2 + i : 3 + i])
        first = jnp.full((128, 1), 65536.0, jnp.float32)
        last = jnp.full((128, 1), -1.0, jnp.float32)
        for j in range(2):
            b_inner, b_col = b_f[4 + j : 5 + j], b_f[6 + j : 7 + j]
            position = a_row * 64.0 + b_col
            slot = jnp.full(square, -1.0, jnp.float32)
            for m in range(kept):
                slot = jnp.where(position == c_code[m], float(m), slot)
            meets = (a_inner == b_inner) & (a_inner > 0.0) & (slot >= 0.0)
            key = (lane_f + 128.0 * j) * 32.0 + slot
            first = jnp.minimum(
                first, jnp.min(jnp.where(meets, key, 65536.0), axis=1, keepdims=True)
            )
            last = jnp.maximum(last, jnp.max(jnp.where(meets, key, -1.0), axis=1, keepdims=True))
        entries.append((i, last, last >= 0.0))
        entries.append((i, first, (last >= 0.0) & (first != last)))
    sub_1 = sub_f[:, :1]
    columns = []
    for n, (i, key, there) in enumerate(entries):
        slot = key - 32.0 * jnp.floor(key * (1.0 / 32.0))
        order = jnp.where(there, slot * 512.0 + (sub_1 + 128.0 * n), 65536.0)
        value = jnp.where(there, (sub_1 + 128.0 * i) * 8192.0 + key, 0.0)
        columns.append((there, slot, order, value))
    lines = [line(order) for _, _, order, _ in columns]
    listed = [jnp.zeros((1, 128), jnp.float32) for _ in range(3)]
    starts = jnp.zeros((1, 128), jnp.float32)
    for there, slot, order, value in columns:
        rank = jnp.zeros((128, 1), jnp.float32)
        for other in lines:
            rank = rank + jnp.sum(jnp.where(other < order, 1.0, 0.0), axis=1, keepdims=True)
        rank = jnp.where(there, rank, -1.0)
        for n in range(3):
            listed[n] = listed[n] + jnp.sum(
                jnp.where(rank == lane_f + 128.0 * n, value, 0.0), axis=0, keepdims=True
            )
        starts = starts + jnp.sum(
            jnp.where(there & (slot < lane_f), 1.0, 0.0), axis=0, keepdims=True
        )
    count = starts[:, kept : kept + 1]
    rows = [
        jnp.where(lane_f[:1] + 128.0 * n < count, listed[n], float(kept)) for n in range(3)
    ] + [jnp.broadcast_to(count, (1, 128)), starts]
    rows = jnp.concatenate(rows + [jnp.zeros((3, 128), jnp.float32)], axis=0)
    return rows.astype(jnp.int32)


def product_kernel(
    list_ref, a_ref, b_ref, out_ref, a_buffer, b_buffer, total, a_sem, b_sem
):
    kept = out_ref.shape[0]
    batches = (list_ref[3, 0] + BATCH - 1) // BATCH

    def listed(at):
        return list_ref[lax.shift_right_logical(at, 7), at & 127]

    def fetch(batch):
        spot = batch & (DEPTH - 1)
        for n in range(BATCH):
            entry = listed(batch * BATCH + n)
            pltpu.make_async_copy(
                a_ref.at[lax.shift_right_logical(entry, 13)], a_buffer.at[spot, n], a_sem.at[spot]
            ).start()
            pltpu.make_async_copy(
                b_ref.at[lax.shift_right_logical(entry, 5) & 255], b_buffer.at[spot, n], b_sem.at[spot]
            ).start()

    def prefetch(batch, carry):
        fetch(batch)
        return carry

    lax.fori_loop(0, jnp.minimum(batches, DEPTH), prefetch, 0)
    total[...] = jnp.zeros_like(total)

    def work(batch, carry):
        spot = batch & (DEPTH - 1)
        pltpu.make_async_copy(a_buffer.at[spot], a_buffer.at[spot], a_sem.at[spot]).wait()
        pltpu.make_async_copy(b_buffer.at[spot], b_buffer.at[spot], b_sem.at[spot]).wait()
        products = [
            jnp.dot(
                a_buffer[spot, n], b_buffer[spot, n], preferred_element_type=jnp.float32
            )
            for n in range(BATCH)
        ]
        for n in range(BATCH):
            slot = listed(batch * BATCH + n) & 31
            total[slot] += products[n]

        @pl.when(batch + DEPTH < batches)
        def _():
            fetch(batch + DEPTH)

        return carry

    lax.fori_loop(0, batches, work, 0)
    out_ref[...] = total[0:kept].astype(out_ref.dtype)


def partial_product(listed, a_all, b_all, kept):
    smem = pl.BlockSpec(memory_space=pltpu.SMEM)
    anywhere = pl.BlockSpec(memory_space=pl.ANY)
    return pl.pallas_call(
        product_kernel,
        out_shape=jax.ShapeDtypeStruct((kept, BLOCK, BLOCK), jnp.bfloat16),
        in_specs=[smem, anywhere, anywhere],
        out_specs=pl.BlockSpec(memory_space=pltpu.VMEM),
        scratch_shapes=[
            pltpu.VMEM((DEPTH, BATCH, BLOCK, BLOCK), jnp.bfloat16),
            pltpu.VMEM((DEPTH, BATCH, BLOCK, BLOCK), jnp.bfloat16),
            pltpu.VMEM((kept + 1, BLOCK, BLOCK), jnp.float32),
            pltpu.SemaphoreType.DMA((DEPTH,)),
            pltpu.SemaphoreType.DMA((DEPTH,)),
        ],
        compiler_params=pltpu.CompilerParams(vmem_limit_bytes=60 << 20),
        name="partial_product",
    )(listed, a_all, b_all)


A_CHUNKS = ((0, 6, 1), (6, 6, 1), (12, 6, -1), (18, 6, -1))
B_CHUNKS = ((0, 5, 1, True), (5, 4, -1, True), (9, 3, 1, False), (12, 4, -1, False))


def gather_kernel(
    a_ref,
    b_ref,
    *rest,
):
    tables, (a_all, b_all, list_ref, m_ref, a_marks, b_marks) = rest[:7], rest[7:13]
    send_sem, recv_sem, own_sem = rest[13:16]
    scalars = rest[16:]
    loads = [
        pltpu.make_async_copy(table, held, own_sem.at[2 + n])
        for n, (table, held) in enumerate(zip(tables, scalars))
    ]
    for load in loads:
        load.start()
    a_index, a_send, a_count, b_index, b_send, b_count, c_index = scalars
    col, row = lax.axis_index("col"), lax.axis_index("row")
    a_ring, b_ring = lax.axis_size("col"), lax.axis_size("row") // 2
    plane, spot = row // b_ring, row % b_ring
    partner = row + b_ring - 2 * b_ring * plane

    def a_peer(way):
        return {"col": lax.rem(col + way + a_ring, a_ring)}

    def b_peer(way):
        return {"row": plane * b_ring + lax.rem(spot + way + b_ring, b_ring)}

    barrier = pltpu.get_barrier_semaphore()
    peers = (a_peer(1), a_peer(-1), b_peer(1), b_peer(-1), {"row": partner})
    for peer in peers:
        pl.semaphore_signal(barrier, inc=1, device_id=peer, device_id_type=MESH)
    pl.semaphore_wait(barrier, len(peers))

    numbers = {}
    sent = []

    def number(name):
        return numbers.setdefault(name, len(numbers))

    def send(name, source, target, peer):
        at = number(name)
        copy = pltpu.make_async_remote_copy(
            src_ref=source,
            dst_ref=target,
            send_sem=send_sem.at[at],
            recv_sem=recv_sem.at[at],
            device_id=peer,
            device_id_type=MESH,
        )
        copy.start()
        sent.append(copy)

    def arrive(name, target, peer):
        at = number(name)
        pltpu.make_async_remote_copy(
            src_ref=target,
            dst_ref=target,
            send_sem=send_sem.at[at],
            recv_sem=recv_sem.at[at],
            device_id=peer,
            device_id_type=MESH,
        ).wait_recv()

    a_pieces = [("marks", lambda o: a_marks.at[o], m_ref, 1, 0.0)]
    for n, (start, size, way) in enumerate(A_CHUNKS):
        a_pieces.append(
            (
                f"a{n}",
                lambda o, start=start, size=size: a_all.at[o, pl.ds(start, size)],
                a_ref.at[pl.ds(start, size)],
                way,
                size,
            )
        )
    b_pieces = [("marks", lambda o: b_marks.at[o], m_ref, 1, 0.0, False)]
    for n, (start, size, way, later) in enumerate(B_CHUNKS):
        b_pieces.append(
            (
                f"b{n}",
                lambda o, start=start, size=size: b_all.at[o, pl.ds(start, size)],
                b_ref.at[pl.ds(start, size)],
                way,
                size,
                later,
            )
        )

    events = []

    def forward_a(piece, way, step, origin, source):
        last = a_ring // 2
        if step < last or (step == last and piece[3] == way):
            send(("a", piece[0], way, step), source, piece[1](origin), a_peer(way))

    def forward_b(piece, way, step, side, origin, source):
        last = b_ring // 2
        if step < last or (step == last and piece[3] == way):
            send(("b", piece[0], way, step, side), source, piece[1](origin), b_peer(way))

    def b_origin(side, place):
        return (plane if side == "own" else 1 - plane) * b_ring + place

    for piece in b_pieces[1:]:
        if not piece[5]:
            send(("x", piece[0], 0, 0), piece[2], piece[1](row), {"row": partner})
    for rank in range(len(A_CHUNKS)):
        for way in (1, -1):
            piece = a_pieces[1:][rank if way == 1 else -1 - rank]
            forward_a(piece, way, 1, col, piece[2])
    for rank in range(len(B_CHUNKS)):
        for way in (1, -1):
            piece = b_pieces[1:][rank if way == 1 else -1 - rank]
            forward_b(piece, way, 1, "own", row, piece[2])
    for piece in b_pieces[1:]:
        if piece[5]:
            send(("x", piece[0], 0, 0), piece[2], piece[1](row), {"row": partner})
    for load in loads:
        load.wait()
    m_ref[...] = own_marks(
        col, row, a_index, a_send.at[0, 0, :, 0], a_count, b_index, b_send.at[0, 0, 0], b_count
    )
    send(("x", "marks", 0, 0), m_ref, b_marks.at[row], {"row": partner})
    for way in (1, -1):
        forward_a(a_pieces[0], way, 1, col, m_ref)
        forward_b(b_pieces[0], way, 1, "own", row, m_ref)
    own = [
        pltpu.make_async_copy(a_ref, a_all.at[col], own_sem.at[0]),
        pltpu.make_async_copy(b_ref, b_all.at[row], own_sem.at[1]),
    ]
    for copy in own:
        copy.start()
    a_marks[col] = m_ref[...]
    b_marks[row] = m_ref[...]

    a_step = sum(piece[4] for piece in a_pieces)
    b_step = sum(piece[4] * (1 if piece[5] else 2) for piece in b_pieces)

    def arrive_a(piece, way, step):
        origin = lax.rem(col - way * step + a_ring, a_ring)
        place = piece[1](origin)
        arrive(("a", piece[0], way, step), place, a_peer(way))
        forward_a(piece, way, step + 1, origin, place)

    def arrive_b(piece, way, step, side):
        origin = b_origin(side, lax.rem(spot - way * step + b_ring, b_ring))
        place = piece[1](origin)
        arrive(("b", piece[0], way, step, side), place, b_peer(way))
        forward_b(piece, way, step + 1, side, origin, place)
        if piece[5]:
            send(("x", piece[0], way, step), place, place, {"row": partner})

    def arrive_x(piece, way, step):
        origin = b_origin("far", lax.rem(spot - way * step + b_ring, b_ring))
        place = piece[1](origin)
        arrive(("x", piece[0], way, step), place, {"row": partner})
        if step == 0 and not piece[5]:
            for on in (1, -1):
                forward_b(piece, on, 1, "far", origin, place)

    def expect(time, event, *about):
        events.append((time, functools.partial(event, *about)))

    for way in (1, -1):
        for step in range(1, a_ring // 2 + 1):
            done = (step - 1) * a_step
            if step < a_ring // 2 or a_pieces[0][3] == way:
                expect(2 * done + a_step, arrive_a, a_pieces[0], way, step)
            for piece in a_pieces[1:][::way]:
                if step < a_ring // 2 or piece[3] == way:
                    done += piece[4]
                    expect(2 * done, arrive_a, piece, way, step)
        for step in range(1, b_ring // 2 + 1):
            done = (step - 1) * b_step
            if step < b_ring // 2 or b_pieces[0][3] == way:
                expect(2 * done + a_step + 0.2, arrive_b, b_pieces[0], way, step, "own")
                expect(2 * done + a_step + 0.4, arrive_b, b_pieces[0], way, step, "far")
            for side in ("own", "far"):
                for piece in b_pieces[1:][::way]:
                    if side == "far" and piece[5]:
                        continue
                    if step < b_ring // 2 or piece[3] == way:
                        done += piece[4]
                        expect(2 * done, arrive_b, piece, way, step, side)
                        if piece[5]:
                            expect(2 * done + 40, arrive_x, piece, way, step)
    x_done = 0
    expect(a_step, arrive_x, b_pieces[0], 0, 0)
    for piece in b_pieces[1:]:
        if not piece[5]:
            x_done += piece[4]
            expect(3 * x_done, arrive_x, piece, 0, 0)
        else:
            expect(60, arrive_x, piece, 0, 0)

    def write_list():
        list_ref[...] = product_list(a_marks, b_marks, c_index)

    expect(2 * (max(a_ring // 2 * a_step, b_ring // 2 * b_step) - min(a_step, b_step)) + a_step + 0.6, write_list)
    for _, event in sorted(events, key=lambda e: e[0]):
        event()
    for copy in own:
        copy.wait()
    for copy in sent:
        copy.wait_send()
    assert len(numbers) <= SEMAPHORES


def gathered(a_own, b_own, a_index, a_send, a_count, b_index, b_send, b_count, c_index):
    anywhere = pl.BlockSpec(memory_space=pl.ANY)
    tables = (a_index, a_send, a_count, b_index, b_send, b_count, c_index)
    cols, rows = lax.axis_size("col"), lax.axis_size("row")
    return pl.pallas_call(
        gather_kernel,
        out_shape=(
            jax.ShapeDtypeStruct((cols,) + a_own.shape, a_own.dtype),
            jax.ShapeDtypeStruct((rows,) + b_own.shape, b_own.dtype),
            jax.ShapeDtypeStruct((8, 128), jnp.int32),
        ),
        in_specs=[anywhere] * (2 + len(tables)),
        out_specs=(anywhere, anywhere, pl.BlockSpec(memory_space=pltpu.VMEM)),
        scratch_shapes=[
            pltpu.VMEM((8, 128), jnp.int32),
            pltpu.VMEM((cols, 8, 128), jnp.int32),
            pltpu.VMEM((rows, 8, 128), jnp.int32),
            pltpu.SemaphoreType.DMA((SEMAPHORES,)),
            pltpu.SemaphoreType.DMA((SEMAPHORES,)),
            pltpu.SemaphoreType.DMA((2 + len(tables),)),
        ]
        + [pltpu.SMEM(table.shape, table.dtype) for table in tables],
        compiler_params=pltpu.CompilerParams(
            collective_id=0, has_side_effects=True, vmem_limit_bytes=60 << 20
        ),
        name="gather_blocks",
    )(a_own, b_own, *tables)


def layer_sum_kernel(
    partial_ref, out_ref, mine, from_sibling, pair, from_far, send_sem, recv_sem, own_sem
):
    layer = lax.axis_index("layer")
    share = out_ref.shape[0]
    piece = share // PIECES
    sibling = {"layer": layer + 1 - 2 * lax.rem(layer, 2)}
    far = {"layer": lax.rem(layer + 2, 4)}
    loads = [
        pltpu.make_async_copy(
            partial_ref.at[pl.ds(owner * share, share)], mine.at[n], own_sem.at[n]
        )
        for n, owner in enumerate((far["layer"], layer))
    ]
    for load in loads:
        load.start()
    barrier = pltpu.get_barrier_semaphore()
    for peer in (sibling, far):
        pl.semaphore_signal(barrier, inc=1, device_id=peer, device_id_type=MESH)
    pl.semaphore_wait(barrier, 2)

    def copy(n, source, target, peer):
        return pltpu.make_async_remote_copy(
            src_ref=source,
            dst_ref=target,
            send_sem=send_sem.at[n],
            recv_sem=recv_sem.at[n],
            device_id=peer,
            device_id_type=MESH,
        )

    on, across = [], []
    for n, owner in enumerate((lax.rem(sibling["layer"] + 2, 4), sibling["layer"])):
        for p in range(PIECES):
            on.append(
                copy(
                    n * PIECES + p,
                    partial_ref.at[pl.ds(owner * share + p * piece, piece)],
                    from_sibling.at[n, pl.ds(p * piece, piece)],
                    sibling,
                )
            )
            on[-1].start()
    loads[0].wait()
    for p in range(PIECES):
        at = pl.ds(p * piece, piece)
        on[p].wait_recv()
        pair[at] = (
            mine[0, at].astype(jnp.float32) + from_sibling[0, at].astype(jnp.float32)
        ).astype(pair.dtype)
        across.append(copy(2 * PIECES + p, pair.at[at], from_far.at[at], far))
        across[-1].start()
    loads[1].wait()
    for p in range(PIECES):
        on[PIECES + p].wait_recv()
    for p in range(PIECES):
        at = pl.ds(p * piece, piece)
        across[p].wait_recv()
        out_ref[at] = (
            mine[1, at].astype(jnp.float32)
            + from_sibling[1, at].astype(jnp.float32)
            + from_far[at].astype(jnp.float32)
        ).astype(out_ref.dtype)
    for sent in on + across:
        sent.wait_send()


def layer_sum(partial):
    share = (partial.shape[0] // lax.axis_size("layer"),) + partial.shape[1:]
    return pl.pallas_call(
        layer_sum_kernel,
        out_shape=jax.ShapeDtypeStruct(share, partial.dtype),
        in_specs=[pl.BlockSpec(memory_space=pl.ANY)],
        out_specs=pl.BlockSpec(memory_space=pltpu.VMEM),
        scratch_shapes=[
            pltpu.VMEM((2,) + share, partial.dtype),
            pltpu.VMEM((2,) + share, partial.dtype),
            pltpu.VMEM(share, partial.dtype),
            pltpu.VMEM(share, partial.dtype),
            pltpu.SemaphoreType.DMA((3 * PIECES,)),
            pltpu.SemaphoreType.DMA((3 * PIECES,)),
            pltpu.SemaphoreType.DMA((2,)),
        ],
        compiler_params=pltpu.CompilerParams(
            collective_id=1, has_side_effects=True, vmem_limit_bytes=60 << 20
        ),
        name="layer_sum",
    )(partial)


def shards(a_blocks, a_index, a_send, a_count, b_blocks, b_index, b_send, b_count, c_index):
    a_all, b_all, listed = gathered(
        a_blocks[0, 0, 0],
        b_blocks[0, 0, 0],
        a_index,
        jnp.transpose(a_send, (0, 1, 4, 2, 3)),
        a_count,
        b_index,
        jnp.transpose(b_send, (0, 1, 2, 4, 3)),
        b_count,
        c_index,
    )
    a_all = a_all.reshape(-1, BLOCK, BLOCK)
    b_all = b_all.reshape(-1, BLOCK, BLOCK)
    partial = partial_product(listed, a_all, b_all, c_index.shape[3])
    return layer_sum(partial)[None, None]


def solution(mesh):
    in_specs = (
        P("row", "col", "layer", None, None, None),
        P("row", "col", "layer", None, None),
        P("row", "col", "layer", None, None),
        P("row", "col", "layer", None),
        P("row", "col", "layer", None, None, None),
        P("row", "col", "layer", None, None),
        P("row", "col", "layer", None, None),
        P("row", "col", "layer", None),
        P("row", "col", None, None),
    )
    out_specs = P("row", "col", "layer", None, None)
    return jax.shard_map(shards, mesh=mesh, in_specs=in_specs, out_specs=out_specs, check_vma=False)
```

time: 113 us -> 98.7 us (0.87)
  other arithmetic: 9.22 us -> 0 us
  local copies, waits for them, and re-layouts: 4.85 us -> 1.62 us
  Pallas kernels: 98.4 us -> 96.4 us
    select_n x7 -> x0, other arithmetic: 3.56 us -> none  [the longest x1 1.15 us: product_list(): return (jnp.where(spots < count, listed, kept), count[None])]
    reduce_sum x4 -> x0, other arithmetic: 2.94 us -> none  [the longest x1 1.85 us: product_list(): jnp.sum(jnp.where((a_row[:, None, None] == c_rows) & (b_col[None, :, None...]
    slice x2 -> x0, local copies, waits for them, and re-layouts: 1.71 us -> none  [the longest x1 0.93 us: shards(): b_code = b_marks[:, 0, a_held:a_held + b_held].reshape(-1)]
    lt x2 -> x0, other arithmetic: 1.32 us -> none  [live_slots(): lax.broadcasted_iota(jnp.int32, send_list.shape, 1) < live_count[:, None]]
    pallas_call x1, Pallas kernels: 12.8 us -> 11.5 us  [layer_sum(): pl.pallas_call(layer_sum_kernel, out_shape=jax.ShapeDtypeStruct(share, pa...]
    unnamed x2 -> x1, local copies, waits for them, and re-layouts: 2.3 us -> 1.62 us
where the time goes in v3:
time: 98.7 us; the launch traced here: 98 us
  Pallas kernels  96.4 us (98%)
  local copies, waits for them, and re-layouts  1.62 us (2%)
    pallas_call x1, Pallas kernels, gathered(): pl.pallas_call(gather_kernel, out_shape=(jax.ShapeDtypeStruct((cols,) + a...  79.5 us
    pallas_call x1, Pallas kernels, layer_sum(): pl.pallas_call(layer_sum_kernel, out_shape=jax.ShapeDtypeStruct(share, pa...  11.5 us
    pallas_call x1, Pallas kernels, partial_product(): pl.pallas_call(product_kernel, out_shape=jax.ShapeDtypeStruct((kept, BLOC...  5.46 us

profile of v3, /device:TPU:1, one launch (start us, length us, event | category | flops | bytes accessed | tf_op | source)
XLA Modules:
  0.0 98.0 jit_solution(4823349848575588177)
XLA Ops:
  0.0 79.5 %gather_blocks.1 = (bf16[8,24,128,128]{3,2,1,0:T(8,128)(2,1)}, bf16[16,16,128,128]{3,2,1,0:T(8,128)(2,1)}, s32[8,128]{1,0:T(8,128)}) custom-call(bf16[24,128,128]{2,1,0:T(8,128)(2,1)} %bitcast.9, bf16[16,128,128]{2,1,0:T(8,128)(2,1)} %bitcast.11, s32[1,1,1,2,24]{4,3,2,1,0:T(2,128)} %rest_0_.1, s32[1,1,3,1,8]{4,3,2,1,0:T(1,128)} %bitcast.12, ...), custom_call_target="tpu_custom_call" | custom-call | tf_op jit(solution)/shard_map/gather_blocks/pallas_call | solution.py:408
  79.5 5.5 %partial_product.1.partial_ref = bf16[24,128,128]{2,1,0:T(8,128)(2,1)} custom-call(s32[8,128]{1,0:T(8,128)} %get-tuple-element.8.list_ref, bf16[192,128,128]{2,1,0:T(8,128)(2,1)} %bitcast.8, bf16[256,128,128]{2,1,0:T(8,128)(2,1)} %bitcast.7), custom_call_target="tpu_custom_call" | custom-call | tf_op jit(solution)/shard_map/partial_product/pallas_call | solution.py:177
  84.9 11.5 %layer_sum.1 = bf16[6,128,128]{2,1,0:T(8,128)(2,1)} custom-call(bf16[24,128,128]{2,1,0:T(8,128)(2,1)} %partial_product.1.partial_ref), custom_call_target="tpu_custom_call" | custom-call | tf_op jit(solution)/shard_map/layer_sum/pallas_call | solution.py:502
  96.4 1.6 %copy.11 = bf16[1,1,6,128,128]{4,3,2,1,0:T(8,128)(2,1)} copy(bf16[1,1,6,128,128]{4,3,2,1,0:T(8,128)(2,1)} %bitcast.10) | data formatting | bytes 393216

commit v4 on v3

--- a/solution.py
+++ b/solution.py
@@ -12,6 +12,10 @@
 DEPTH = 4
 SEMAPHORES = 128
 PIECES = 3
+MARKS_A = 12.1
+MARKS_B = 12.1
+LIST_AT = 157.0
+B_PRIORITY = 0
 MESH = pl.DeviceIdType.MESH
 
 
@@ -96,11 +100,11 @@
         slot = key - 32.0 * jnp.floor(key * (1.0 / 32.0))
         order = jnp.where(there, slot * 512.0 + (sub_1 + 128.0 * n), 65536.0)
         value = jnp.where(there, (sub_1 + 128.0 * i) * 8192.0 + key, 0.0)
-        columns.append((there, slot, order, value))
-    lines = [line(order) for _, _, order, _ in columns]
+        columns.append((there, order, value))
+    lines = [line(order) for _, order, _ in columns]
     listed = [jnp.zeros((1, 128), jnp.float32) for _ in range(3)]
-    starts = jnp.zeros((1, 128), jnp.float32)
-    for there, slot, order, value in columns:
+    count = jnp.zeros((1, 1), jnp.float32)
+    for there, order, value in columns:
         rank = jnp.zeros((128, 1), jnp.float32)
         for other in lines:
             rank = rank + jnp.sum(jnp.where(other < order, 1.0, 0.0), axis=1, keepdims=True)
@@ -109,36 +113,41 @@
             listed[n] = listed[n] + jnp.sum(
                 jnp.where(rank == lane_f + 128.0 * n, value, 0.0), axis=0, keepdims=True
             )
-        starts = starts + jnp.sum(
-            jnp.where(there & (slot < lane_f), 1.0, 0.0), axis=0, keepdims=True
-        )
-    count = starts[:, kept : kept + 1]
-    rows = [
-        jnp.where(lane_f[:1] + 128.0 * n < count, listed[n], float(kept)) for n in range(3)
-    ] + [jnp.broadcast_to(count, (1, 128)), starts]
-    rows = jnp.concatenate(rows + [jnp.zeros((3, 128), jnp.float32)], axis=0)
-    return rows.astype(jnp.int32)
+        count = count + jnp.sum(jnp.where(there, 1.0, 0.0), axis=0, keepdims=True)
+    rows = jnp.concatenate(
+        [jnp.where(lane_f[:1] + 128.0 * n < count, listed[n], float(kept)) for n in range(3)]
+        + [jnp.broadcast_to(count, (1, 128)), jnp.zeros((4, 128), jnp.float32)],
+        axis=0,
+    ).astype(jnp.int32)
+    return (
+        lax.shift_right_logical(rows, 13),
+        lax.shift_right_logical(rows, 5) & 255,
+        rows & 31,
+        rows,
+    )
 
 
 def product_kernel(
     list_ref, a_ref, b_ref, out_ref, a_buffer, b_buffer, total, a_sem, b_sem
 ):
     kept = out_ref.shape[0]
-    batches = (list_ref[3, 0] + BATCH - 1) // BATCH
-
-    def listed(at):
-        return list_ref[lax.shift_right_logical(at, 7), at & 127]
+    batches = lax.div(list_ref[3, 3, 0] + (BATCH - 1), BATCH)
+
+    def listed(part, batch):
+        first = batch * BATCH
+        row, lane = lax.shift_right_logical(first, 7), first & 127
+        return [list_ref[part, row, lane + n] for n in range(BATCH)]
 
     def fetch(batch):
         spot = batch & (DEPTH - 1)
+        a_spots, b_spots = listed(0, batch), listed(1, batch)
         for n in range(BATCH):
-            entry = listed(batch * BATCH + n)
             pltpu.make_async_copy(
-                a_ref.at[lax.shift_right_logical(entry, 13)], a_buffer.at[spot, n], a_sem.at[spot]
+                a_ref.at[a_spots[n]], a_buffer.at[spot, n], a_sem.at[spot]
             ).start()
             pltpu.make_async_copy(
-                b_ref.at[lax.shift_right_logical(entry, 5) & 255], b_buffer.at[spot, n], b_sem.at[spot]
-            ).start()
+                b_ref.at[b_spots[n]], b_buffer.at[spot, n], b_sem.at[spot]
+            ).start(B_PRIORITY)
 
     def prefetch(batch, carry):
         fetch(batch)
@@ -157,9 +166,9 @@
             )
             for n in range(BATCH)
         ]
+        slots = listed(2, batch)
         for n in range(BATCH):
-            slot = listed(batch * BATCH + n) & 31
-            total[slot] += products[n]
+            total[slots[n]] += products[n]
 
         @pl.when(batch + DEPTH < batches)
         def _():
@@ -299,17 +308,18 @@
     for piece in b_pieces[1:]:
         if not piece[5]:
             send(("x", piece[0], 0, 0), piece[2], piece[1](row), {"row": partner})
-    for rank in range(len(A_CHUNKS)):
-        for way in (1, -1):
-            piece = a_pieces[1:][rank if way == 1 else -1 - rank]
-            forward_a(piece, way, 1, col, piece[2])
-    for rank in range(len(B_CHUNKS)):
-        for way in (1, -1):
-            piece = b_pieces[1:][rank if way == 1 else -1 - rank]
-            forward_b(piece, way, 1, "own", row, piece[2])
-    for piece in b_pieces[1:]:
-        if piece[5]:
-            send(("x", piece[0], 0, 0), piece[2], piece[1](row), {"row": partner})
+
+    def leave(ranks):
+        for rank in ranks:
+            for way in (1, -1):
+                if rank < len(A_CHUNKS):
+                    piece = a_pieces[1:][rank if way == 1 else -1 - rank]
+                    forward_a(piece, way, 1, col, piece[2])
+                if rank < len(B_CHUNKS):
+                    piece = b_pieces[1:][rank if way == 1 else -1 - rank]
+                    forward_b(piece, way, 1, "own", row, piece[2])
+
+    leave(range(1))
     for load in loads:
         load.wait()
     m_ref[...] = own_marks(
@@ -319,6 +329,10 @@
     for way in (1, -1):
         forward_a(a_pieces[0], way, 1, col, m_ref)
         forward_b(b_pieces[0], way, 1, "own", row, m_ref)
+    leave(range(1, max(len(A_CHUNKS), len(B_CHUNKS))))
+    for piece in b_pieces[1:]:
+        if piece[5]:
+            send(("x", piece[0], 0, 0), piece[2], piece[1](row), {"row": partner})
     own = [
         pltpu.make_async_copy(a_ref, a_all.at[col], own_sem.at[0]),
         pltpu.make_async_copy(b_ref, b_all.at[row], own_sem.at[1]),
@@ -360,7 +374,7 @@
         for step in range(1, a_ring // 2 + 1):
             done = (step - 1) * a_step
             if step < a_ring // 2 or a_pieces[0][3] == way:
-                expect(2 * done + a_step, arrive_a, a_pieces[0], way, step)
+                expect(2 * done + MARKS_A, arrive_a, a_pieces[0], way, step)
             for piece in a_pieces[1:][::way]:
                 if step < a_ring // 2 or piece[3] == way:
                     done += piece[4]
@@ -368,8 +382,8 @@
         for step in range(1, b_ring // 2 + 1):
             done = (step - 1) * b_step
             if step < b_ring // 2 or b_pieces[0][3] == way:
-                expect(2 * done + a_step + 0.2, arrive_b, b_pieces[0], way, step, "own")
-                expect(2 * done + a_step + 0.4, arrive_b, b_pieces[0], way, step, "far")
+                expect(2 * done + MARKS_B + 0.2, arrive_b, b_pieces[0], way, step, "own")
+                expect(2 * done + MARKS_B + 0.4, arrive_b, b_pieces[0], way, step, "far")
             for side in ("own", "far"):
                 for piece in b_pieces[1:][::way]:
                     if side == "far" and piece[5]:
@@ -380,7 +394,7 @@
                         if piece[5]:
                             expect(2 * done + 40, arrive_x, piece, way, step)
     x_done = 0
-    expect(a_step, arrive_x, b_pieces[0], 0, 0)
+    expect(MARKS_B, arrive_x, b_pieces[0], 0, 0)
     for piece in b_pieces[1:]:
         if not piece[5]:
             x_done += piece[4]
@@ -389,9 +403,10 @@
             expect(60, arrive_x, piece, 0, 0)
 
     def write_list():
-        list_ref[...] = product_list(a_marks, b_marks, c_index)
-
-    expect(2 * (max(a_ring // 2 * a_step, b_ring // 2 * b_step) - min(a_step, b_step)) + a_step + 0.6, write_list)
+        for n, part in enumerate(product_list(a_marks, b_marks, c_index)):
+            list_ref[n] = part
+
+    expect(LIST_AT, write_list)
     for _, event in sorted(events, key=lambda e: e[0]):
         event()
     for copy in own:
@@ -410,7 +425,7 @@
         out_shape=(
             jax.ShapeDtypeStruct((cols,) + a_own.shape, a_own.dtype),
             jax.ShapeDtypeStruct((rows,) + b_own.shape, b_own.dtype),
-            jax.ShapeDtypeStruct((8, 128), jnp.int32),
+            jax.ShapeDtypeStruct((4, 8, 128), jnp.int32),
         ),
         in_specs=[anywhere] * (2 + len(tables)),
         out_specs=(anywhere, anywhere, pl.BlockSpec(memory_space=pltpu.VMEM)),
@@ -431,10 +446,10 @@
 
 
 def layer_sum_kernel(
-    partial_ref, out_ref, mine, from_sibling, pair, from_far, send_sem, recv_sem, own_sem
+    partial_ref, near_ref, from_far, mine, from_sibling, pair, near, send_sem, recv_sem, own_sem
 ):
     layer = lax.axis_index("layer")
-    share = out_ref.shape[0]
+    share = near_ref.shape[0]
     piece = share // PIECES
     sibling = {"layer": layer + 1 - 2 * lax.rem(layer, 2)}
     far = {"layer": lax.rem(layer + 2, 4)}
@@ -484,40 +499,44 @@
         across[-1].start()
     loads[1].wait()
     for p in range(PIECES):
+        at = pl.ds(p * piece, piece)
         on[PIECES + p].wait_recv()
+        near[at] = mine[1, at].astype(jnp.float32) + from_sibling[1, at].astype(jnp.float32)
+    store = pltpu.make_async_copy(near, near_ref, own_sem.at[2])
+    store.start()
     for p in range(PIECES):
-        at = pl.ds(p * piece, piece)
         across[p].wait_recv()
-        out_ref[at] = (
-            mine[1, at].astype(jnp.float32)
-            + from_sibling[1, at].astype(jnp.float32)
-            + from_far[at].astype(jnp.float32)
-        ).astype(out_ref.dtype)
+    store.wait()
     for sent in on + across:
         sent.wait_send()
 
 
 def layer_sum(partial):
     share = (partial.shape[0] // lax.axis_size("layer"),) + partial.shape[1:]
-    return pl.pallas_call(
+    anywhere = pl.BlockSpec(memory_space=pl.ANY)
+    near, far = pl.pallas_call(
         layer_sum_kernel,
-        out_shape=jax.ShapeDtypeStruct(share, partial.dtype),
-        in_specs=[pl.BlockSpec(memory_space=pl.ANY)],
-        out_specs=pl.BlockSpec(memory_space=pltpu.VMEM),
+        out_shape=(
+            jax.ShapeDtypeStruct(share, jnp.float32),
+            jax.ShapeDtypeStruct(share, partial.dtype),
+        ),
+        in_specs=[anywhere],
+        out_specs=(anywhere, anywhere),
         scratch_shapes=[
             pltpu.VMEM((2,) + share, partial.dtype),
             pltpu.VMEM((2,) + share, partial.dtype),
             pltpu.VMEM(share, partial.dtype),
-            pltpu.VMEM(share, partial.dtype),
+            pltpu.VMEM(share, jnp.float32),
             pltpu.SemaphoreType.DMA((3 * PIECES,)),
             pltpu.SemaphoreType.DMA((3 * PIECES,)),
-            pltpu.SemaphoreType.DMA((2,)),
+            pltpu.SemaphoreType.DMA((3,)),
         ],
         compiler_params=pltpu.CompilerParams(
-            collective_id=1, has_side_effects=True, vmem_limit_bytes=60 << 20
+            collective_id=1, has_side_effects=True, vmem_limit_bytes=53 << 20
         ),
         name="layer_sum",
     )(partial)
+    return (near + far.astype(jnp.float32)).astype(partial.dtype)
 
 
 def shards(a_blocks, a_index, a_send, a_count, b_blocks, b_index, b_send, b_count, c_index):

time: 98.7 us -> 97.6 us (0.989)
  local copies, waits for them, and re-layouts: 1.62 us -> 0 us
    unnamed x1 -> x0, local copies, waits for them, and re-layouts: 1.62 us -> none
    pallas_call x1, Pallas kernels: 79.5 us -> 78 us  [gathered(): pl.pallas_call(gather_kernel, out_shape=(jax.ShapeDtypeStruct((cols,) + a...]
    pallas_call x1, Pallas kernels: 11.5 us -> 12.7 us  [layer_sum(): pl.pallas_call(layer_sum_kernel, out_shape=(jax.ShapeDtypeStruct(share, j...]
where the time goes in v4:
time: 97.6 us; the launch traced here: 97 us
  Pallas kernels  96.2 us (99%)
    pallas_call x1, Pallas kernels, gathered(): pl.pallas_call(gather_kernel, out_shape=(jax.ShapeDtypeStruct((cols,) + a...  78 us
    pallas_call x1, Pallas kernels, layer_sum(): pl.pallas_call(layer_sum_kernel, out_shape=(jax.ShapeDtypeStruct(share, j...  12.7 us
    pallas_call x1, Pallas kernels, partial_product(): pl.pallas_call(product_kernel, out_shape=jax.ShapeDtypeStruct((kept, BLOC...  5.55 us

profile of v4, /device:TPU:1, one launch (start us, length us, event | category | flops | bytes accessed | tf_op | source)
XLA Modules:
  0.0 97.0 jit_solution(3269399808454191762)
XLA Ops:
  0.0 78.0 %gather_blocks.1 = (bf16[8,24,128,128]{3,2,1,0:T(8,128)(2,1)}, bf16[16,16,128,128]{3,2,1,0:T(8,128)(2,1)}, s32[4,8,128]{2,1,0:T(8,128)}) custom-call(bf16[24,128,128]{2,1,0:T(8,128)(2,1)} %bitcast.10, bf16[16,128,128]{2,1,0:T(8,128)(2,1)} %bitcast.11, s32[1,1,1,2,24]{4,3,2,1,0:T(2,128)} %rest_0_.1, s32[1,1,3,1,8]{4,3,2,1,0:T(1,128)} %bitcast.12, ...), custom_call_target="tpu_custom_call" | custom-call | tf_op jit(solution)/shard_map/gather_blocks/pallas_call | solution.py:423
  78.0 5.5 %partial_product.1.partial_ref = bf16[24,128,128]{2,1,0:T(8,128)(2,1)} custom-call(s32[4,8,128]{2,1,0:T(8,128)} %get-tuple-element.10.list_ref, bf16[192,128,128]{2,1,0:T(8,128)(2,1)} %bitcast.9, bf16[256,128,128]{2,1,0:T(8,128)(2,1)} %bitcast.8), custom_call_target="tpu_custom_call" | custom-call | tf_op jit(solution)/shard_map/partial_product/pallas_call | solution.py:186
  83.6 12.7 %layer_sum.1 = (f32[6,128,128]{2,1,0:T(8,128)S(1)}, bf16[6,128,128]{2,1,0:T(8,128)(2,1)S(1)}) custom-call(bf16[24,128,128]{2,1,0:T(8,128)(2,1)} %partial_product.1.partial_ref), custom_call_target="tpu_custom_call" | custom-call | tf_op jit(solution)/shard_map/layer_sum/pallas_call | solution.py:517
  96.3 0.7 fusion

commit v5 on v4

--- a/solution.py
+++ b/solution.py
@@ -9,7 +9,7 @@
 
 BLOCK = 128
 BATCH = 8
-DEPTH = 4
+DEPTH = 8
 SEMAPHORES = 128
 PIECES = 3
 MARKS_A = 12.1

time: 97.6 us -> 96.6 us (0.990)
  no operation moved by 1% of the time
where the time goes in v5:
time: 96.6 us; the launch traced here: 96.2 us
  Pallas kernels  95.4 us (99%)
    pallas_call x1, Pallas kernels, gathered(): pl.pallas_call(gather_kernel, out_shape=(jax.ShapeDtypeStruct((cols,) + a...  78 us
    pallas_call x1, Pallas kernels, layer_sum(): pl.pallas_call(layer_sum_kernel, out_shape=(jax.ShapeDtypeStruct(share, j...  12.1 us
    pallas_call x1, Pallas kernels, partial_product(): pl.pallas_call(product_kernel, out_shape=jax.ShapeDtypeStruct((kept, BLOC...  5.39 us

profile of v5, /device:TPU:1, one launch (start us, length us, event | category | flops | bytes accessed | tf_op | source)
XLA Modules:
  0.0 96.2 jit_solution(4409541192544806259)
XLA Ops:
  0.0 78.0 %gather_blocks.1 = (bf16[8,24,128,128]{3,2,1,0:T(8,128)(2,1)}, bf16[16,16,128,128]{3,2,1,0:T(8,128)(2,1)}, s32[4,8,128]{2,1,0:T(8,128)}) custom-call(bf16[24,128,128]{2,1,0:T(8,128)(2,1)} %bitcast.10, bf16[16,128,128]{2,1,0:T(8,128)(2,1)} %bitcast.11, s32[1,1,1,2,24]{4,3,2,1,0:T(2,128)} %rest_0_.1, s32[1,1,3,1,8]{4,3,2,1,0:T(1,128)} %bitcast.12, ...), custom_call_target="tpu_custom_call" | custom-call | tf_op jit(solution)/shard_map/gather_blocks/pallas_call | solution.py:423
  78.0 5.4 %partial_product.1.partial_ref = bf16[24,128,128]{2,1,0:T(8,128)(2,1)} custom-call(s32[4,8,128]{2,1,0:T(8,128)} %get-tuple-element.10.list_ref, bf16[192,128,128]{2,1,0:T(8,128)(2,1)} %bitcast.9, bf16[256,128,128]{2,1,0:T(8,128)(2,1)} %bitcast.8), custom_call_target="tpu_custom_call" | custom-call | tf_op jit(solution)/shard_map/partial_product/pallas_call | solution.py:186
  83.4 12.1 %layer_sum.1 = (f32[6,128,128]{2,1,0:T(8,128)S(1)}, bf16[6,128,128]{2,1,0:T(8,128)(2,1)S(1)}) custom-call(bf16[24,128,128]{2,1,0:T(8,128)(2,1)} %partial_product.1.partial_ref), custom_call_target="tpu_custom_call" | custom-call | tf_op jit(solution)/shard_map/layer_sum/pallas_call | solution.py:517
  95.5 0.7 fusion
